TPU v7x, 256 devices: a whole 4x4x8 slice. The times are simulated.
256 devices in a mesh: grp: 64 (over z, x_lo, y), blk: 4 (over x_hi, core).
Axes of the slice: x: 4 (x_hi: 2, x_lo: 2; x = x_hi * 2 + x_lo), y: 4, z: 8, core: 2. Of those that a mesh axis runs over, the one named last changes fastest.
Arguments:
- field_phase: float32 [6, 131072], P(None, ('grp', 'blk')), may hold values from -10 to 10
- field_mass: float32 [131072], P(('grp', 'blk')), may hold values from 0.2 to 5
- old_force: float32 [6, 16384], P(None, ('grp', 'blk')), may hold values from -6 to 6
- target_slot: int32 [101, 16384], P(None, ('grp', 'blk')), may hold values from 0 to 13311, as said below
- target_star: int32 [101, 16384], P(None, ('grp', 'blk')), may hold values from 0 to 511
Outputs:
- reg_force: float32 [6, 16384], P(None, ('grp', 'blk'))
- irr_force: float32 [6, 16384], P(None, ('grp', 'blk'))
- new_state: float32 [6, 16384], P(None, ('grp', 'blk'))
Inputs may be any that keep to these rules, and one draw needn't show every extreme that they name: `target_slot`: within the 64 columns of one device all slots differ; slot // 52 is the index, grp-major over grp and blk, of the device that holds the star, so at most 52 entries of one device go to one owner, and some owners receive exactly 52 from every device.
All inputs are finite; a program needn't handle non-finite values.
Results may differ from a plain program's by a relative error of at most 0.0003.
Values sent between devices are 32-bit elements; how exact they have to be, the bound alone decides.
A program may use at most 128 MiB of HBM per device.

v0:
```python
import math

import jax
import jax.numpy as jnp
from jax import lax
from jax.sharding import PartitionSpec as P

soften_sq = 0.01
step_length = 0.5


def passed_along(x, axis, by):
    count = lax.axis_size(axis)
    return lax.ppermute(x, axis, [(i, (i + by) % count) for i in range(count)])


def pair_block(receivers, emitters):
    separation = emitters[0:3, None, :] - receivers[0:3, :, None]
    rel_velocity = emitters[3:6, None, :] - receivers[3:6, :, None]
    dist_sq = soften_sq + jnp.sum(separation * separation, axis=0)
    inverse = lax.rsqrt(dist_sq)
    weight = emitters[6][None, :] * inverse * inverse * inverse
    radial = 3.0 * jnp.sum(separation * rel_velocity, axis=0) / dist_sq
    pull_sum = jnp.sum(weight[None] * separation, axis=2)
    jerk_sum = jnp.sum(weight[None] * (rel_velocity - radial[None] * separation), axis=2)
    return jnp.concatenate([pull_sum, jerk_sum], axis=0)


def pair_sum(receivers, emitters):
    row_total = receivers.shape[1]
    tile_rows = math.gcd(row_total, 256)
    tiles = receivers.reshape(6, row_total // tile_rows, tile_rows).transpose(1, 0, 2)
    emit_total = emitters.shape[1]
    emit_rows = math.gcd(emit_total, 1024)
    emit_blocks = emitters.reshape(7, emit_total // emit_rows, emit_rows).transpose(1, 0, 2)

    def single_tile(block_rows):

        def add_block(total, emit_piece):
            return (total + pair_block(block_rows, emit_piece), None)

        start = jnp.zeros((6, tile_rows), jnp.float32)
        total, unused = lax.scan(add_block, start, emit_blocks)
        return total

    result = lax.map(single_tile, tiles)
    return result.transpose(1, 0, 2).reshape(6, row_total)


def neighbour_sum(receivers, emitters):
    separation = emitters[0:3] - receivers[0:3, None, :]
    rel_velocity = emitters[3:6] - receivers[3:6, None, :]
    dist_sq = soften_sq + jnp.sum(separation * separation, axis=0)
    inverse = lax.rsqrt(dist_sq)
    weight = emitters[6] * inverse * inverse * inverse
    radial = 3.0 * jnp.sum(separation * rel_velocity, axis=0) / dist_sq
    pull_sum = jnp.sum(weight[None] * separation, axis=1)
    jerk_sum = jnp.sum(weight[None] * (rel_velocity - radial[None] * separation), axis=1)
    return jnp.concatenate([pull_sum, jerk_sum], axis=0)


def corrector(home_state, regular, irregular, old_force):
    accel_new = regular[0:3] + irregular[0:3]
    jerk_new = regular[3:6] + irregular[3:6]
    difference = old_force[0:3] - accel_new
    snap_term = -6.0 * difference - step_length * (4.0 * old_force[3:6] + 2.0 * jerk_new)
    crackle_term = 12.0 * difference + 6.0 * step_length * (old_force[3:6] + jerk_new)
    step_square = step_length * step_length
    position = home_state[0:3] + step_square / 24.0 * snap_term + step_square / 120.0 * crackle_term
    velocity = home_state[3:6] + step_length / 6.0 * snap_term + step_length / 24.0 * crackle_term
    return jnp.concatenate([position, velocity], axis=0)


def per_device(field_phase, field_mass, old_force, target_slot, target_star):
    target_cols = target_slot.shape[0]
    active_rows = target_slot.shape[1]
    group_count = lax.axis_size("grp")
    loop_count = lax.axis_size("blk")
    device_count = group_count * loop_count
    local_stars = field_phase.shape[1]
    star_total = local_stars * device_count
    star_table = jnp.concatenate([field_phase, field_mass[None, :]], axis=0)
    target_count = target_cols * active_rows
    bucket_size = 2 * ((target_count + device_count - 1) // device_count)
    slot_flat = target_slot.reshape(target_count)
    star_flat = target_star.reshape(target_count)
    requested = jnp.zeros((device_count * bucket_size,), jnp.int32).at[slot_flat].set(star_flat)
    requested = requested.reshape(group_count, loop_count, bucket_size)
    incoming = lax.all_to_all(
        lax.all_to_all(requested, "grp", split_axis=0, concat_axis=0, tiled=True),
        "blk",
        split_axis=1,
        concat_axis=1,
        tiled=True,
    )
    looked_up = jnp.take(star_table, incoming.reshape(device_count * bucket_size), axis=1)
    looked_up = looked_up.reshape(7, group_count, loop_count, bucket_size)
    returned = lax.all_to_all(
        lax.all_to_all(looked_up, "grp", split_axis=1, concat_axis=1, tiled=True),
        "blk",
        split_axis=2,
        concat_axis=2,
        tiled=True,
    )
    fetched = jnp.take(returned.reshape(7, device_count * bucket_size), slot_flat, axis=1)
    fetched = fetched.reshape(7, target_cols, active_rows)
    own_state = fetched[0:6, 0, :]
    irregular = neighbour_sum(own_state, fetched[:, 1:, :]) / (target_cols - 1)
    group_block = lax.all_gather(own_state, "grp", axis=1, tiled=True)
    running = jnp.zeros_like(group_block)
    moving = group_block
    for circuit in range(loop_count):
        running = running + pair_sum(moving, star_table)
        parcel = passed_along(jnp.concatenate([moving, running], axis=0), "blk", 1)
        moving = parcel[0:6]
        running = parcel[6:12]
    row_offset = lax.axis_index("grp") * active_rows
    home_state = lax.dynamic_slice_in_dim(moving, row_offset, active_rows, 1)
    summed = lax.psum(running, "grp")
    regular = lax.dynamic_slice_in_dim(summed, row_offset, active_rows, 1)
    regular = regular / star_total
    return (regular, irregular, corrector(home_state, regular, irregular, old_force))


def solution(mesh):
    in_specs = (
        P(None, ("grp", "blk")),
        P(("grp", "blk")),
        P(None, ("grp", "blk")),
        P(None, ("grp", "blk")),
        P(None, ("grp", "blk")),
    )
    out_specs = (P(None, ("grp", "blk")), P(None, ("grp", "blk")), P(None, ("grp", "blk")))
    return jax.shard_map(
        per_device, mesh=mesh, in_specs=in_specs, out_specs=out_specs, check_vma=False
    )
```

profile of v0, /device:TPU:4, one launch (start us, length us, event | category | flops | bytes accessed | tf_op | source)
XLA Modules:
  0.0 1011.9 jit_solution(18103508663828550580)
XLA Ops:
  7.2 0.9 copy.102
  8.2 0.9 copy.103
  9.2 31.2 %scatter_custom_fusion = s32[13312]{0:T(1024)S(1)} fusion(s32[6464]{0:T(1024)S(1)} %fusion.27, s32[6464]{0:T(1024)S(1)} %reshape.357, s32[]{:T(128)} %constant.114.clone.1), kind=kCustom, calls=%fused_computation.106 | custom fusion | bytes 53252 | tf_op jit(solution)/shard_map/scatter | solution.py:87
  40.7 23.1 %all_to_all.20 = s32[64,1,208]{2,1,0:T(1,128)S(1)} all-to-all(s32[64,1,208]{2,1,0:T(1,128)S(1)} %reshape.368), channel_id=1, replica_groups=mesh['grp'=64,'blk'=4] {'grp'}, dimensions={0} | all-to-all | bytes 106496 | tf_op jit(solution)/shard_map/all_to_all | solution.py:90
  66.2 4.8 all-to-all-start.1
  71.2 2.0 all-to-all-done.1
  74.5 44.3 %gather_fusion = f32[13312,7]{1,0:T(8,128)} fusion(f32[7,512]{0,1:T(8,128)S(1)} %copy.107, s32[13312]{0:T(1024)S(1)} %broadcast_clamp_fusion), kind=kCustom, calls=%fused_computation | custom fusion | bytes 798720 | tf_op jit(solution)/shard_map/jit(_take)/gather | solution.py:96
  118.8 5.0 copy.108
  123.8 1.5 gather.13
  125.7 2.3 reshape.372
  128.0 4.6 all-to-all-start.2
  132.7 15.8 %all-to-all-done.2 = f32[64,1,1456]{2,1,0:T(1,128)S(1)} async-done(((f32[64,1,1456]{2,1,0:T(1,128)}), f32[64,1,1456]{2,1,0:T(1,128)S(1)}, u32[]{:S(2)}, u32[]{:S(2)}) %all-to-all-start.2) | async-done | bytes 372768 | tf_op jit(solution)/shard_map/all_to_all | solution.py:99
  149.0 1.6 reduce.8
  151.5 1.2 reshape.374
  152.7 6.8 all-to-all-start.3
  160.2 4.9 all-to-all-done.3
  165.1 1.7 reduce.9
  167.6 1.1 reshape.328
  168.7 4.6 copy.112
  173.4 13.4 %gather_fusion.1 = f32[6464,7]{1,0:T(8,128)S(1)} fusion(f32[7,13312]{0,1:T(8,128)} %copy.112, s32[7168]{0:T(1024)S(1)} %pad_clamp_fusion), kind=kCustom, calls=%fused_computation.1 | custom fusion | bytes 387840 | tf_op jit(solution)/shard_map/jit(_take)/gather | solution.py:105
  186.8 2.1 copy.113
  190.1 164.5 %all-gather = f32[6,1,4096]{0,1,2:T(1,128)S(1)} all-gather(f32[6,1,64]{0,1,2:T(1,128)S(1)} %copy.114), channel_id=2, replica_groups=mesh['grp'=64,'blk'=4] {'grp'}, dimensions={2}, use_global_device_ids=true | all-gather | bytes 99840 | tf_op jit(solution)/shard_map/all_gather | solution.py:109
  354.6 2.0 copy.115
  356.7 21.9 %while.36 = (s32[]{:T(128)}, f32[16,6,256]{2,1,0:T(8,128)S(1)}, f32[1,7,512]{2,1,0:T(8,128)S(1)}, f32[16,6,256]{2,0,1:T(8,128)S(1)}, s32[]{:T(128)}, /*index=5*/s32[]{:T(128)}, s32[]{}) while((s32[]{:T(128)}, f32[16,6,256]{2,1,0:T(8,128)S(1)}, f32[1,7,512]{2,1,0:T(8,128)S(1)}, f32[16,6,256]{2,0,1:T(8,128)S(1)}, s32[]{:T(128)}, ...), condition=%wide.region_6.7_spmd, body=%wide.region_1.6_spmd.sunk | while | flops 6029315 | bytes 4309093 | solution.py:46
  378.7 7.3 collective-permute-done
  386.0 21.6 %while.37 = (s32[]{:T(128)}, f32[16,6,256]{2,1,0:T(8,128)S(1)}, f32[1,7,512]{2,1,0:T(8,128)S(1)}, f32[16,6,256]{2,1,0:T(8,128)S(1)}, s32[]{:T(128)}, /*index=5*/s32[]{:T(128)}, s32[]{}) while((s32[]{:T(128)}, f32[16,6,256]{2,1,0:T(8,128)S(1)}, f32[1,7,512]{2,1,0:T(8,128)S(1)}, f32[16,6,256]{2,1,0:T(8,128)S(1)}, s32[]{:T(128)}, ...), condition=%wide.region_12.13_spmd, body=%wide.region_7.12_spmd.sunk | while | flops 6029315 | bytes 4296805 | solution.py:46
  408.1 7.0 collective-permute-done.1
  415.1 21.6 %while.38 = (s32[]{:T(128)}, f32[16,6,256]{2,1,0:T(8,128)S(1)}, f32[1,7,512]{2,1,0:T(8,128)S(1)}, f32[16,6,256]{2,1,0:T(8,128)S(1)}, s32[]{:T(128)}, /*index=5*/s32[]{:T(128)}, s32[]{}) while((s32[]{:T(128)}, f32[16,6,256]{2,1,0:T(8,128)S(1)}, f32[1,7,512]{2,1,0:T(8,128)S(1)}, f32[16,6,256]{2,1,0:T(8,128)S(1)}, s32[]{:T(128)}, ...), condition=%wide.region_18.19_spmd, body=%wide.region_13.18_spmd.sunk | while | flops 6029315 | bytes 4296805 | solution.py:46
  437.2 7.2 collective-permute-done.2
  444.5 21.6 %while.39 = (s32[]{:T(128)}, f32[16,6,256]{2,1,0:T(8,128)S(1)}, f32[1,7,512]{2,1,0:T(8,128)S(1)}, f32[16,6,256]{2,1,0:T(8,128)S(1)}, s32[]{:T(128)}, /*index=5*/s32[]{:T(128)}, s32[]{}) while((s32[]{:T(128)}, f32[16,6,256]{2,1,0:T(8,128)S(1)}, f32[1,7,512]{2,1,0:T(8,128)S(1)}, f32[16,6,256]{2,1,0:T(8,128)S(1)}, s32[]{:T(128)}, ...), condition=%wide.region_24.25_spmd, body=%wide.region_19.24_spmd.sunk | while | flops 6029315 | bytes 4296805 | solution.py:46
  466.5 7.0 collective-permute-done.3
  474.3 529.3 %all-reduce.2.cloned.1.call-done = f32[6,4096]{1,0:T(8,128)} async-done(((f32[6,4096]{1,0:T(8,128)}), f32[6,4096]{1,0:T(8,128)}) %all-reduce.2.cloned.1.call-update) | async-done | bytes 98320 | tf_op jit(solution)/shard_map/psum | solution.py:119
  (540 shorter events, 95.6 us)
Async XLA Ops:
  7.2 63.8 %copy-start.4 = (f32[512]{0:T(512)S(1)}, f32[512]{0:T(512)}, u32[]{:S(2)}) copy-start(f32[512]{0:T(512)} %param.14) | copy-start | bytes 6148
  7.2 63.8 %copy-start.1 = (f32[6,512]{1,0:T(8,128)S(1)}, f32[6,512]{1,0:T(8,128)}, u32[]{:S(2)}) copy-start(f32[6,512]{1,0:T(8,128)} %param.13) | copy-start | bytes 36868
  66.2 6.9 all-to-all-start.1
  128.0 20.4 %all-to-all-start.2 = ((f32[64,1,1456]{2,1,0:T(1,128)}), f32[64,1,1456]{2,1,0:T(1,128)S(1)}, u32[]{:S(2)}, u32[]{:S(2)}) async-start(f32[64,1,1456]{2,1,0:T(1,128)} %reshape.372), calls=%async_computation.2 | async-start | bytes 786432 | tf_op jit(solution)/shard_map/all_to_all | solution.py:99
  151.1 8.5 copy-start
  152.7 12.4 %all-to-all-start.3 = ((f32[4,1,23296]{2,1,0:T(1,128)}), f32[4,1,23296]{2,1,0:T(1,128)S(1)}, u32[]{:S(2)}, u32[]{:S(2)}) async-start(f32[4,1,23296]{2,1,0:T(1,128)} %reshape.374), calls=%async_computation.3 | async-start | bytes 745472 | tf_op jit(solution)/shard_map/all_to_all | solution.py:98
  159.6 844.1 %all-reduce.2.cloned.1.call-start = ((), (), s32[]{:S(2)}) async-start(), calls=%async_computation.4 | async-start | bytes 262144 | tf_op jit(solution)/shard_map/psum | solution.py:119
  378.6 7.4 collective-permute-start
  407.7 7.4 collective-permute-start.1
  436.8 7.6 collective-permute-start.2
  466.1 538.3 %copy-start.5 = (f32[6,64]{1,0:T(8,128)S(1)}, f32[6,64]{1,0:T(8,128)}, u32[]{:S(2)}) copy-start(f32[6,64]{1,0:T(8,128)} %param.15) | copy-start | bytes 4612
  466.2 7.4 collective-permute-start.3
  474.3 530.7 %copy-start.3 = (f32[6,64]{1,0:T(8,128)}, f32[6,64]{1,0:T(8,128)S(1)}, u32[]{:S(2)}) copy-start(f32[6,64]{1,0:T(8,128)S(1)} %get-tuple-element.288) | copy-start | bytes 4612
  1004.4 0.6 copy-start.2
Sparse Core Ops, SparseCore 0:
  474.4 529.2 all-reduce.1
where the time goes:
time: 1010 us
  waiting for transfers between devices  580 us (57%)
  blocking collectives  188 us (19%)
  local copies, waits for them, and re-layouts  118 us (12%)
  other arithmetic  90.4 us (9%)
  starting transfers between devices  16.8 us (2%)
  between operations  14.5 us (1%)
    psum x1, waiting for transfers between devices, per_device(): summed = lax.psum(running, 'grp')  529 us
    all_gather x1, blocking collectives, per_device(): group_block = lax.all_gather(own_state, 'grp', axis=1, tiled=True)  165 us
    gather x3, local copies, waits for them, and re-layouts, per_device(): jnp.take(star_table, incoming.reshape(device_count * bucket_size), axis=1)  50.8 us
    reduce_sum x64, other arithmetic, pair_block(): pull_sum = jnp.sum(weight[None] * separation, axis=2)  48.2 us
    scatter x1, local copies, waits for them, and re-layouts, per_device(): jnp.zeros((device_count * bucket_size,), jnp.int32).at[slot_flat]  31.2 us
    ppermute x4, waiting for transfers between devices, passed_along(): return lax.ppermute(x, axis, [(i, (i + by) % count) for i in range(count)])  28.5 us
    reduce_sum x64, other arithmetic, pair_block(): dist_sq = soften_sq + jnp.sum(separation * separation, axis=0)  23.2 us
    all_to_all x1, blocking collectives, per_device(): lax.all_to_all(requested, 'grp', split_axis=0, concat_axis=0, tiled=True)  23.1 us
  transfers between devices with their start and end apart: 8, of which 8 were waited for; matrix products, arithmetic and copies ran while one was open for 0% of the time, Pallas kernels for 0%

commit v1 on v0

v1 whole, which is shorter than its diff:
```python
import functools

import jax
import jax.numpy as jnp
from jax import lax
from jax.experimental import pallas as pl
from jax.experimental.pallas import tpu as pltpu
from jax.sharding import PartitionSpec as P

MESH = pl.DeviceIdType.MESH
NT = (((1,), (1,)), ((), ()))
F32 = jnp.float32
BF16 = jnp.bfloat16

SOFTEN = 0.01
STEP = 0.5
NZ, NX, NY = 8, 4, 4
STAR_DEV = 512
ACT_DEV = 64
NBR = 100
MOST = 52
OWNERS = 256
STARS = OWNERS * STAR_DEV
PAIRS = OWNERS // 2
HALF_ROWS = 51
BLOCK_ROWS = 32
UNROLL = 4


def gather_kernel(phase_ref, mass_ref, out_ref, z_send, z_recv, a_send, a_recv, b_send, b_recv, c_send, c_recv):
    grp = lax.axis_index("grp")
    blk = lax.axis_index("blk")
    z = grp // 8
    x_lo = (grp // 4) % 2
    y = grp % 4
    x = (blk // 2) * 2 + x_lo
    core = blk % 2
    a = core * x + (1 - core) * y
    b = core * y + (1 - core) * x

    def device(cz, ca, cb, cc):
        cx = core * ca + (1 - core) * cb
        cy = core * cb + (1 - core) * ca
        return (cz * 8 + (cx % 2) * 4 + cy, (cx // 2) * 2 + cc)

    a_up, a_down = (a + 1) % 4, (a + 3) % 4
    b_up, b_down = (b + 1) % 4, (b + 3) % 4
    partners = [device((z + k) % NZ, a, b, core) for k in range(1, NZ)]
    partners += [device(z, a_up, b, core), device(z, a_down, b, core)]
    partners += [device(z, a, b_up, core), device(z, a, b_down, core)]
    partners += [device(z, a, b, 1 - core)]

    out_ref[core, b, a, z, 0:6, :] = phase_ref[...]
    out_ref[core, b, a, z, 6:7, :] = mass_ref[...]
    out_ref[core, b, a, z, 7:8, :] = jnp.ones((1, STAR_DEV), F32)

    barrier = pltpu.get_barrier_semaphore()
    for partner in partners:
        pl.semaphore_signal(barrier, inc=1, device_id=partner, device_id_type=MESH)
    pl.semaphore_wait(barrier, len(partners))

    started = []

    def send(part, send_sem, recv_sem, target):
        copy = pltpu.make_async_remote_copy(
            src_ref=part, dst_ref=part, send_sem=send_sem, recv_sem=recv_sem, device_id=target, device_id_type=MESH
        )
        copy.start()
        started.append(copy)

    def await_recv(part, send_sem, recv_sem):
        pltpu.make_async_remote_copy(
            src_ref=part, dst_ref=part, send_sem=send_sem, recv_sem=recv_sem,
            device_id=partners[-1], device_id_type=MESH,
        ).wait_recv()

    def block(bb, aa):
        return out_ref.at[core, bb, aa]

    def part(bb, aa, half):
        return out_ref.at[core, bb, aa, pl.ds(4 * half, 4)]

    for k in range(1, NZ):
        send(out_ref.at[core, b, a, z], z_send.at[k], z_recv.at[k], partners[k - 1])
    for k in range(1, NZ):
        await_recv(out_ref.at[core, b, a, (z + NZ - k) % NZ], z_send.at[k], z_recv.at[k])

    to_a_up, to_a_down = partners[7], partners[8]
    to_b_up, to_b_down = partners[9], partners[10]
    other = partners[11]

    def send_core(bb, aa, n):
        send(block(bb, aa), c_send.at[n], c_recv.at[n], other)

    def send_b(aa, n):
        send(block(b, aa), b_send.at[n, 0], b_recv.at[n, 0], to_b_up)
        send(block(b, aa), b_send.at[n, 1], b_recv.at[n, 1], to_b_down)

    def near_b(aa, n):
        await_recv(block(b_down, aa), b_send.at[n, 0], b_recv.at[n, 0])
        send(part(b_down, aa, 0), b_send.at[n, 2], b_recv.at[n, 2], to_b_up)
        send_core(b_down, aa, 4 * n + 1)
        await_recv(block(b_up, aa), b_send.at[n, 1], b_recv.at[n, 1])
        send(part(b_up, aa, 1), b_send.at[n, 3], b_recv.at[n, 3], to_b_down)
        send_core(b_up, aa, 4 * n + 2)

    def far_b(aa, n):
        far = (b + 2) % 4
        await_recv(part(far, aa, 0), b_send.at[n, 2], b_recv.at[n, 2])
        await_recv(part(far, aa, 1), b_send.at[n, 3], b_recv.at[n, 3])
        send_core(far, aa, 4 * n + 3)

    send(block(b, a), a_send.at[0], a_recv.at[0], to_a_up)
    send(block(b, a), a_send.at[1], a_recv.at[1], to_a_down)
    send_b(a, 0)
    send_core(b, a, 0)

    await_recv(block(b, a_down), a_send.at[0], a_recv.at[0])
    send(part(b, a_down, 0), a_send.at[2], a_recv.at[2], to_a_up)
    send_b(a_down, 1)
    send_core(b, a_down, 4)
    await_recv(block(b, a_up), a_send.at[1], a_recv.at[1])
    send(part(b, a_up, 1), a_send.at[3], a_recv.at[3], to_a_down)
    send_b(a_up, 2)
    send_core(b, a_up, 8)
    a_far = (a + 2) % 4
    near_b(a, 0)
    await_recv(part(b, a_far, 0), a_send.at[2], a_recv.at[2])
    await_recv(part(b, a_far, 1), a_send.at[3], a_recv.at[3])
    send_b(a_far, 3)
    send_core(b, a_far, 12)
    near_b(a_down, 1)
    far_b(a, 0)
    near_b(a_up, 2)
    far_b(a_down, 1)
    near_b(a_far, 3)
    far_b(a_up, 2)
    far_b(a_far, 3)

    oa, ob = b, a
    for n, da in enumerate((0, 3, 1, 2)):
        for m, db in enumerate((0, 3, 1, 2)):
            await_recv(out_ref.at[1 - core, (ob + db) % 4, (oa + da) % 4], c_send.at[4 * n + m], c_recv.at[4 * n + m])
    for copy in started:
        copy.wait_send()


def gather_table(phase, mass):
    return pl.pallas_call(
        gather_kernel,
        out_shape=jax.ShapeDtypeStruct((2, 4, 4, NZ, 8, STAR_DEV), F32),
        in_specs=[pl.BlockSpec(memory_space=pltpu.VMEM)] * 2,
        out_specs=pl.BlockSpec(memory_space=pltpu.VMEM),
        scratch_shapes=[
            pltpu.SemaphoreType.DMA((8,)),
            pltpu.SemaphoreType.DMA((8,)),
            pltpu.SemaphoreType.DMA((4,)),
            pltpu.SemaphoreType.DMA((4,)),
            pltpu.SemaphoreType.DMA((4, 4)),
            pltpu.SemaphoreType.DMA((4, 4)),
            pltpu.SemaphoreType.DMA((16,)),
            pltpu.SemaphoreType.DMA((16,)),
        ],
        compiler_params=pltpu.CompilerParams(
            collective_id=0, has_side_effects=True, vmem_limit_bytes=24 * 2**20
        ),
        name="gather_table",
    )(phase, mass)


def split2(v):
    high = v.astype(BF16)
    return high, (v - high.astype(F32)).astype(BF16)


def split3_rows(v):
    high = v.astype(BF16).astype(F32)
    rest = v - high
    middle = rest.astype(BF16).astype(F32)
    return jnp.concatenate([high, middle, rest - middle], axis=0).astype(BF16)


def table_place(owner):
    core = owner & 1
    x = ((owner >> 1) & 1) * 2 + ((owner >> 4) & 1)
    y = (owner >> 2) & 3
    z = owner >> 5
    ab = jnp.where(core == 1, y * 4 + x, x * 4 + y)
    return core * 128 + ab * 8 + z


def force_kernel(
    table_ref, slot_ref, star_ref, old_ref, reg_ref, irr_ref, new_ref,
    own_smem, own_vec, place_scr, code_scr, column_scr, req1, req2, fetched, terms, own_b, acc, copy_sem,
):
    lane = lax.broadcasted_iota(jnp.int32, (56, 128), 1)
    row = lax.broadcasted_iota(jnp.int32, (56, 128), 0)
    place_scr[...] = jnp.zeros_like(place_scr)
    code_scr[...] = jnp.zeros_like(code_scr)
    place_scr[0:HALF_ROWS, 0:ACT_DEV] = slot_ref[0:HALF_ROWS, :]
    place_scr[0:NBR + 1 - HALF_ROWS, ACT_DEV:128] = slot_ref[HALF_ROWS:NBR + 1, :]
    code_scr[0:HALF_ROWS, 0:ACT_DEV] = star_ref[0:HALF_ROWS, :]
    code_scr[0:NBR + 1 - HALF_ROWS, ACT_DEV:128] = star_ref[HALF_ROWS:NBR + 1, :]
    slot = place_scr[...]
    star = code_scr[...]
    owner = (slot * 20165) >> 20
    within = slot - owner * MOST
    place = table_place(owner)
    active = lane & 63
    listed = (row < NBR + 1 - HALF_ROWS) | ((row == NBR + 1 - HALF_ROWS) & (lane < ACT_DEV))
    neighbour = listed & ((row > 0) | (lane >= ACT_DEV))
    place_scr[...] = jnp.where(neighbour, place >> 1, -1)
    column_scr[...] = within + 64 * (place & 1)
    code_scr[...] = star + active * 512

    own_vec[...] = jnp.zeros_like(own_vec)
    own_vec[0:1, :] = place[0:1, :] * 512 + star[0:1, :]
    fill = pltpu.make_async_copy(own_vec, own_smem, copy_sem)
    fill.start()
    fill.wait()
    lane8 = lax.broadcasted_iota(jnp.int32, (8, 128), 1)
    own = jnp.zeros((8, 128), F32)
    for i in range(ACT_DEV):
        code = own_smem[0, i]
        shard = code >> 9
        start = pl.multiple_of(((code >> 7) & 3) * 128, 128)
        tile = table_ref[shard, :, pl.ds(start, 128)]
        turned = pltpu.roll(tile, (i + 128 - (code & 127)) & 127, 1)
        own = jnp.where(lane8 == i, turned, own)
    own_columns = jnp.transpose(own)
    for c in range(6):
        own_b[c] = jnp.broadcast_to(own_columns[0:ACT_DEV, c:c + 1], (ACT_DEV, 128))

    iota128 = lax.broadcasted_iota(jnp.int32, (128, 128), 0)
    req1[...] = jnp.zeros_like(req1)
    req2[...] = jnp.zeros_like(req2)

    def add_requests(r, carry):
        rows_a, rows_1, rows_2 = [], [], []
        for k in range(2):
            line = 2 * r + k
            place_row = place_scr[pl.ds(line, 1), :]
            column_row = column_scr[pl.ds(line, 1), :]
            code_row = code_scr[pl.ds(line, 1), :]
            first = ((code_row & 127) + 128).astype(F32)
            second = (code_row >> 7).astype(F32)
            rows_a.append(jnp.where(iota128 == place_row, 1.0, 0.0).astype(BF16))
            hit = iota128 == column_row
            rows_1.append(jnp.where(hit, first, 0.0).astype(BF16))
            rows_2.append(jnp.where(hit, second, 0.0).astype(BF16))
        onehot = jnp.concatenate(rows_a, axis=1)
        req1[...] += lax.dot_general(onehot, jnp.concatenate(rows_1, axis=1), NT, preferred_element_type=F32)
        req2[...] += lax.dot_general(onehot, jnp.concatenate(rows_2, axis=1), NT, preferred_element_type=F32)
        return carry

    lax.fori_loop(0, (HALF_ROWS + 1) // 2, add_requests, 0)

    def fetch(pair, carry):
        first = jnp.broadcast_to(req1[pl.ds(pair, 1), :], (8, 128)).astype(jnp.int32)
        second = jnp.broadcast_to(req2[pl.ds(pair, 1), :], (8, 128)).astype(jnp.int32)
        index = first & 127
        quarter = second & 3
        both = []
        for h in range(2):
            got = None
            for t in range(4):
                tile = table_ref[2 * pair + h, :, t * 128:t * 128 + 128]
                column = jnp.take_along_axis(tile, index, axis=1)
                got = column if t == 0 else jnp.where(quarter == t, column, got)
            both.append(got)
        fetched[pl.ds(pl.multiple_of(pair * 8, 8), 8), :] = jnp.where(lane8 < 64, both[0], both[1])
        return carry

    lax.fori_loop(0, PAIRS, fetch, 0, unroll=4)

    def neighbour_terms(g, carry):
        base = pl.multiple_of(g * 64, 64)
        lines = pl.ds(pl.multiple_of(g * 8, 8), 8)
        first = req1[lines, :]
        index = req2[lines, :].astype(jnp.int32) >> 2
        star_rows = [fetched[pl.ds(base + c, 8, stride=8), :] for c in range(7)]
        own_rows = [
            jnp.take_along_axis(jnp.broadcast_to(own[c:c + 1, :], (8, 128)), index, axis=1) for c in range(6)
        ]
        d = [star_rows[c] - own_rows[c] for c in range(3)]
        w = [star_rows[c] - own_rows[c] for c in range(3, 6)]
        q = SOFTEN + (d[0] * d[0] + d[1] * d[1] + d[2] * d[2])
        dw = d[0] * w[0] + d[1] * w[1] + d[2] * w[2]
        inverse = lax.rsqrt(q)
        square = inverse * inverse
        weight = jnp.where(first > 0.5, star_rows[6] * inverse * square, 0.0)
        radial = 3.0 * dw * square
        for c in range(3):
            terms[pl.ds(base + c, 8, stride=8), :] = weight * d[c]
            terms[pl.ds(base + 3 + c, 8, stride=8), :] = weight * (w[c] - radial * d[c])
        terms[pl.ds(base + 6, 8, stride=8), :] = jnp.zeros((8, 128), F32)
        terms[pl.ds(base + 7, 8, stride=8), :] = jnp.zeros((8, 128), F32)
        return carry

    lax.fori_loop(0, PAIRS // 8, neighbour_terms, 0)

    iota64 = lax.broadcasted_iota(jnp.int32, (ACT_DEV, 128), 0)

    def add_terms(p, carry):
        lefts, rights = [], []
        for k in range(2):
            pair = 2 * p + k
            t = terms[pl.ds(pl.multiple_of(pair * 8, 8), 8), :]
            high = t.astype(BF16).astype(F32)
            lefts.append(jnp.concatenate([high, t - high], axis=0).astype(BF16))
            index = req2[pl.ds(pair, 1), :].astype(jnp.int32) >> 2
            rights.append(jnp.where(iota64 == index, 1.0, 0.0).astype(BF16))
        return carry + lax.dot_general(
            jnp.concatenate(lefts, axis=1), jnp.concatenate(rights, axis=1), NT, preferred_element_type=F32
        )

    sums = lax.fori_loop(0, PAIRS // 2, add_terms, jnp.zeros((16, ACT_DEV), F32), unroll=2)
    irregular = (sums[0:6, :] + sums[8:14, :]) / NBR

    acc[...] = jnp.zeros_like(acc)

    def add_shards(g, carry):
        for u in range(UNROLL):
            shard = g * UNROLL + u
            whole = table_ref[shard]
            emit = split3_rows(whole * whole[6:7, :])
            for ib in range(ACT_DEV // BLOCK_ROWS):
                rows = slice(ib * BLOCK_ROWS, (ib + 1) * BLOCK_ROWS)
                quarters = []
                for t in range(4):
                    lanes = slice(t * 128, t * 128 + 128)
                    d = [table_ref[shard, c:c + 1, lanes] - own_b[c, rows, :] for c in range(3)]
                    w = [table_ref[shard, c:c + 1, lanes] - own_b[c, rows, :] for c in range(3, 6)]
                    q = (d[0] * d[0] + d[1] * d[1]) + (d[2] * d[2] + SOFTEN)
                    dw = d[0] * w[0] + d[1] * w[1] + d[2] * w[2]
                    inverse = lax.rsqrt(q)
                    square = inverse * inverse
                    v = square * inverse
                    u_ = dw * (v * square)
                    quarters.append(split2(v) + split2(u_))
                weights = jnp.concatenate(
                    [jnp.concatenate([part[k] for part in quarters], axis=1) for k in range(4)], axis=0
                )
                acc[ib] += lax.dot_general(weights, emit, NT, preferred_element_type=F32)
        return carry

    lax.fori_loop(0, OWNERS // UNROLL, add_shards, 0)
    v_sums, u_sums = [], []
    for ib in range(ACT_DEV // BLOCK_ROWS):
        a = acc[ib]
        v_sums.append(a[0:BLOCK_ROWS] + a[BLOCK_ROWS:2 * BLOCK_ROWS])
        u_sums.append(a[2 * BLOCK_ROWS:3 * BLOCK_ROWS] + a[3 * BLOCK_ROWS:])
    pad = jnp.zeros((128 - ACT_DEV, 24), F32)

    def to_rows(s):
        s = jnp.concatenate(s + [pad], axis=0)
        s = jnp.concatenate([s, jnp.zeros((128, 104), F32)], axis=1)
        s = jnp.transpose(s)[:, 0:ACT_DEV]
        return s[0:8] + s[8:16] + s[16:24]

    v_rows = to_rows(v_sums)
    u_rows = to_rows(u_sums)
    home = own[:, 0:ACT_DEV]
    v_terms = v_rows - home * v_rows[7:8]
    u_terms = u_rows - home * u_rows[7:8]
    accel = v_terms[0:3] / STARS
    jerk = (v_terms[3:6] - 3.0 * u_terms[0:3]) / STARS

    old = old_ref[...]
    accel_new = accel + irregular[0:3]
    jerk_new = jerk + irregular[3:6]
    difference = old[0:3] - accel_new
    snap = -6.0 * difference - STEP * (4.0 * old[3:6] + 2.0 * jerk_new)
    crackle = 12.0 * difference + 6.0 * STEP * (old[3:6] + jerk_new)
    reg_ref[0:3, :] = accel
    reg_ref[3:6, :] = jerk
    irr_ref[...] = irregular
    new_ref[0:3, :] = home[0:3] + STEP * STEP / 24.0 * snap + STEP * STEP / 120.0 * crackle
    new_ref[3:6, :] = home[3:6] + STEP / 6.0 * snap + STEP / 24.0 * crackle


def forces(table, target_slot, target_star, old_force):
    vmem = pl.BlockSpec(memory_space=pltpu.VMEM)
    out = jax.ShapeDtypeStruct((6, ACT_DEV), F32)
    return pl.pallas_call(
        force_kernel,
        out_shape=(out, out, out),
        in_specs=[vmem] * 4,
        out_specs=(vmem,) * 3,
        scratch_shapes=[
            pltpu.SMEM((8, 128), jnp.int32),
            pltpu.VMEM((8, 128), jnp.int32),
            pltpu.VMEM((56, 128), jnp.int32),
            pltpu.VMEM((56, 128), jnp.int32),
            pltpu.VMEM((56, 128), jnp.int32),
            pltpu.VMEM((PAIRS, 128), F32),
            pltpu.VMEM((PAIRS, 128), F32),
            pltpu.VMEM((PAIRS * 8, 128), F32),
            pltpu.VMEM((PAIRS * 8, 128), F32),
            pltpu.VMEM((6, ACT_DEV, 128), F32),
            pltpu.VMEM((ACT_DEV // BLOCK_ROWS, 4 * BLOCK_ROWS, 24), F32),
            pltpu.SemaphoreType.DMA,
        ],
        compiler_params=pltpu.CompilerParams(vmem_limit_bytes=32 * 2**20),
        name="forces",
    )(table, target_slot, target_star, old_force)


def per_device(field_phase, field_mass, old_force, target_slot, target_star):
    table = gather_table(field_phase, field_mass.reshape(1, STAR_DEV))
    table = table.reshape(OWNERS, 8, STAR_DEV)
    return forces(table, target_slot, target_star, old_force)


def solution(mesh):
    split = P(None, ("grp", "blk"))
    return jax.shard_map(
        per_device,
        mesh=mesh,
        in_specs=(split, P(("grp", "blk")), split, split, split),
        out_specs=(split, split, split),
        check_vma=False,
    )
```

time: 1010 us -> 105 us (0.10)
  the two profiles are of different devices: /device:TPU:4 before, /device:TPU:1 now
where the time goes in v1:
time: 105 us; the launch traced here: 104 us
  Pallas kernels  101 us (96%)
  local copies, waits for them, and re-layouts  3.13 us (3%)
    pallas_call x1, Pallas kernels, forces(): pl.pallas_call(force_kernel, out_shape=(out, out, out), in_specs=[vmem] *...  65.2 us
    pallas_call x1, Pallas kernels, gather_table(): pl.pallas_call(gather_kernel, out_shape=jax.ShapeDtypeStruct((2, 4, 4, NZ...  35.5 us
    unnamed x8, local copies, waits for them, and re-layouts  3.13 us

profile of v1, /device:TPU:1, one launch (start us, length us, event | category | flops | bytes accessed | tf_op | source)
XLA Modules:
  0.0 104.5 jit_solution(11164407969329020357)
XLA Ops:
  0.6 0.0 copy-start.1
  0.6 0.9 copy.8.slot_ref
  1.5 0.9 copy.9.star_ref
  2.4 0.0 copy-start
  2.4 0.7 copy-done
  3.1 0.0 copy-start.2
  3.1 0.7 copy-done.2
  3.8 35.5 %gather_table.1 = f32[2,4,4,8,8,512]{5,4,3,2,1,0:T(8,128)S(1)} custom-call(f32[6,512]{1,0:T(8,128)S(1)} %copy-done, f32[1,512]{1,0:T(1,128)S(1)} %bitcast.3), custom_call_target="tpu_custom_call" | custom-call | tf_op jit(solution)/shard_map/gather_table/pallas_call | solution.py:149
  39.3 0.0 copy-done.1
  39.3 65.2 %forces.1 = (f32[6,64]{1,0:T(8,128)}, f32[6,64]{1,0:T(8,128)}, f32[6,64]{1,0:T(8,128)}) custom-call(f32[256,8,512]{2,1,0:T(8,128)S(1)} %bitcast.2, s32[101,64]{1,0:T(8,128)S(1)} %copy.8.slot_ref, s32[101,64]{1,0:T(8,128)S(1)} %copy.9.star_ref, f32[6,64]{1,0:T(8,128)S(1)} %copy-done.1), custom_call_target="tpu_custom_call" | custom-call | tf_op jit(solution)/shard_map/forces/pallas_call | solution.py:385
Async XLA Ops:
  0.6 38.6 %copy-start.1 = (f32[6,64]{1,0:T(8,128)S(1)}, f32[6,64]{1,0:T(8,128)}, u32[]{:S(2)}) copy-start(f32[6,64]{1,0:T(8,128)} %old_ref.1) | copy-start | bytes 4612
  2.4 0.7 copy-start
  3.1 0.7 copy-start.2

commit v2 on v1

v2 whole, which is shorter than its diff:
```python
import functools

import jax
import jax.numpy as jnp
from jax import lax
from jax.experimental import pallas as pl
from jax.experimental.pallas import tpu as pltpu
from jax.sharding import PartitionSpec as P

MESH = pl.DeviceIdType.MESH
NT = (((1,), (1,)), ((), ()))
F32 = jnp.float32
BF16 = jnp.bfloat16

SOFTEN = 0.01
STEP = 0.5
NZ, NX, NY = 8, 4, 4
STAR_DEV = 512
ACT_DEV = 64
NBR = 100
MOST = 52
OWNERS = 256
STARS = OWNERS * STAR_DEV
PAIRS = OWNERS // 2
HALF_ROWS = 51
UNROLL = 8


def table_place(owner):
    core = owner & 1
    x = ((owner >> 1) & 1) * 2 + ((owner >> 4) & 1)
    y = (owner >> 2) & 3
    z = owner >> 5
    ab = jnp.where(core == 1, y * 4 + x, x * 4 + y)
    return core * 128 + ab * 8 + z


def build_requests(slot_ref, star_ref, req_ref, own_ref, place_scr, code_scr, column_scr):
    lane = lax.broadcasted_iota(jnp.int32, (56, 128), 1)
    row = lax.broadcasted_iota(jnp.int32, (56, 128), 0)
    place_scr[...] = jnp.zeros_like(place_scr)
    code_scr[...] = jnp.zeros_like(code_scr)
    place_scr[0:HALF_ROWS, 0:ACT_DEV] = slot_ref[0:HALF_ROWS, :]
    place_scr[0:NBR + 1 - HALF_ROWS, ACT_DEV:128] = slot_ref[HALF_ROWS:NBR + 1, :]
    code_scr[0:HALF_ROWS, 0:ACT_DEV] = star_ref[0:HALF_ROWS, :]
    code_scr[0:NBR + 1 - HALF_ROWS, ACT_DEV:128] = star_ref[HALF_ROWS:NBR + 1, :]
    slot = place_scr[...]
    star = code_scr[...]
    owner = (slot * 20165) >> 20
    within = slot - owner * MOST
    place = table_place(owner)
    active = lane & 63
    listed = (row < NBR + 1 - HALF_ROWS) | ((row == NBR + 1 - HALF_ROWS) & (lane < ACT_DEV))
    neighbour = listed & ((row > 0) | (lane >= ACT_DEV))
    place_scr[...] = jnp.where(neighbour, place >> 1, -1)
    column_scr[...] = within + 64 * (place & 1)
    code_scr[...] = star + active * 512
    own_ref[...] = jnp.broadcast_to(place[0:1, :] * 512 + star[0:1, :], (8, 128))

    iota128 = lax.broadcasted_iota(jnp.int32, (128, 128), 0)
    req_ref[...] = jnp.zeros_like(req_ref)

    def add_requests(r, carry):
        rows_a, rows_b = [], []
        for k in range(8):
            line = 8 * r + k
            place_row = place_scr[pl.ds(line, 1), :]
            column_row = column_scr[pl.ds(line, 1), :]
            code_row = code_scr[pl.ds(line, 1), :]
            first = ((code_row & 127) + 128).astype(F32)
            second = (code_row >> 7).astype(F32)
            rows_a.append(jnp.where(iota128 == place_row, 1.0, 0.0).astype(BF16))
            hit = iota128 == column_row
            rows_b.append(
                jnp.concatenate([jnp.where(hit, first, 0.0), jnp.where(hit, second, 0.0)], axis=0).astype(BF16)
            )
        placed = lax.dot_general(
            jnp.concatenate(rows_a, axis=1), jnp.concatenate(rows_b, axis=1), NT, preferred_element_type=F32
        )
        req_ref[0] += placed[:, 0:128]
        req_ref[1] += placed[:, 128:256]
        return carry

    lax.fori_loop(0, 7, add_requests, 0)


def gather_kernel(
    phase_hbm, mass_hbm, slot_hbm, star_hbm, out_ref, req_ref, own_ref,
    phase_ref, mass_ref, slot_ref, star_ref, place_scr, code_scr, column_scr,
    in_sem, z_send, z_recv, a_send, a_recv, b_send, b_recv, c_send, c_recv,
):
    loads = [
        pltpu.make_async_copy(source, target, in_sem.at[n])
        for n, (source, target) in enumerate(
            ((phase_hbm, phase_ref), (mass_hbm, mass_ref), (slot_hbm, slot_ref), (star_hbm, star_ref))
        )
    ]
    for load in loads:
        load.start()
    grp = lax.axis_index("grp")
    blk = lax.axis_index("blk")
    z = grp // 8
    x_lo = (grp // 4) % 2
    y = grp % 4
    x = (blk // 2) * 2 + x_lo
    core = blk % 2
    a = core * x + (1 - core) * y
    b = core * y + (1 - core) * x

    def device(cz, ca, cb, cc):
        cx = core * ca + (1 - core) * cb
        cy = core * cb + (1 - core) * ca
        return (cz * 8 + (cx % 2) * 4 + cy, (cx // 2) * 2 + cc)

    a_up, a_down = (a + 1) % 4, (a + 3) % 4
    b_up, b_down = (b + 1) % 4, (b + 3) % 4
    partners = [device((z + k) % NZ, a, b, core) for k in range(1, NZ)]
    partners += [device(z, a_up, b, core), device(z, a_down, b, core)]
    partners += [device(z, a, b_up, core), device(z, a, b_down, core)]
    partners += [device(z, a, b, 1 - core), device(z, (a + 2) % 4, b, core)]

    loads[0].wait()
    loads[1].wait()

    for t in range(4):
        lanes = slice(t * 128, t * 128 + 128)
        out_ref[core, b, a, z, t, 0:6, :] = phase_ref[:, lanes]
        out_ref[core, b, a, z, t, 6:7, :] = mass_ref[:, lanes]
        out_ref[core, b, a, z, t, 7:8, :] = jnp.ones((1, 128), F32)

    barrier = pltpu.get_barrier_semaphore()
    for partner in partners:
        pl.semaphore_signal(barrier, inc=1, device_id=partner, device_id_type=MESH)
    pl.semaphore_wait(barrier, len(partners))

    started = []

    def send(part, send_sem, recv_sem, target):
        copy = pltpu.make_async_remote_copy(
            src_ref=part, dst_ref=part, send_sem=send_sem, recv_sem=recv_sem, device_id=target, device_id_type=MESH
        )
        copy.start()
        started.append(copy)

    def await_recv(part, send_sem, recv_sem):
        pltpu.make_async_remote_copy(
            src_ref=part, dst_ref=part, send_sem=send_sem, recv_sem=recv_sem,
            device_id=partners[11], device_id_type=MESH,
        ).wait_recv()

    def block(bb, aa):
        return out_ref.at[core, bb, aa]

    def part(bb, aa, half):
        return out_ref.at[core, bb, aa, pl.ds(4 * half, 4)]

    for k in range(1, NZ):
        send(out_ref.at[core, b, a, z], z_send.at[k], z_recv.at[k], partners[k - 1])
    loads[2].wait()
    loads[3].wait()
    build_requests(slot_ref, star_ref, req_ref, own_ref, place_scr, code_scr, column_scr)
    for k in range(1, NZ):
        await_recv(out_ref.at[core, b, a, (z + NZ - k) % NZ], z_send.at[k], z_recv.at[k])

    to_a_up, to_a_down = partners[7], partners[8]
    to_b_up, to_b_down = partners[9], partners[10]
    other = partners[11]

    def send_core(bb, aa, n):
        send(block(bb, aa), c_send.at[n], c_recv.at[n], other)

    def send_b(aa, n):
        send(block(b, aa), b_send.at[n, 0], b_recv.at[n, 0], to_b_up)
        send(block(b, aa), b_send.at[n, 1], b_recv.at[n, 1], to_b_down)

    def near_b(aa, n):
        await_recv(block(b_down, aa), b_send.at[n, 0], b_recv.at[n, 0])
        send(part(b_down, aa, 0), b_send.at[n, 2], b_recv.at[n, 2], to_b_up)
        send_core(b_down, aa, 4 * n + 1)
        await_recv(block(b_up, aa), b_send.at[n, 1], b_recv.at[n, 1])
        send(part(b_up, aa, 1), b_send.at[n, 3], b_recv.at[n, 3], to_b_down)
        send_core(b_up, aa, 4 * n + 2)

    def far_b(aa, n):
        far = (b + 2) % 4
        await_recv(part(far, aa, 0), b_send.at[n, 2], b_recv.at[n, 2])
        await_recv(part(far, aa, 1), b_send.at[n, 3], b_recv.at[n, 3])
        send_core(far, aa, 4 * n + 3)

    send(block(b, a), a_send.at[0], a_recv.at[0], to_a_up)
    send(block(b, a), a_send.at[1], a_recv.at[1], to_a_down)
    send(block(b, a), a_send.at[2], a_recv.at[2], partners[12])
    send_b(a, 0)
    send_core(b, a, 0)

    await_recv(block(b, a_down), a_send.at[0], a_recv.at[0])
    send_b(a_down, 1)
    send_core(b, a_down, 4)
    await_recv(block(b, a_up), a_send.at[1], a_recv.at[1])
    send_b(a_up, 2)
    send_core(b, a_up, 8)
    a_far = (a + 2) % 4
    near_b(a, 0)
    await_recv(block(b, a_far), a_send.at[2], a_recv.at[2])
    send_b(a_far, 3)
    send_core(b, a_far, 12)
    near_b(a_down, 1)
    far_b(a, 0)
    near_b(a_up, 2)
    far_b(a_down, 1)
    near_b(a_far, 3)
    far_b(a_up, 2)
    far_b(a_far, 3)

    oa, ob = b, a
    for n, da in enumerate((0, 3, 1, 2)):
        for m, db in enumerate((0, 3, 1, 2)):
            await_recv(out_ref.at[1 - core, (ob + db) % 4, (oa + da) % 4], c_send.at[4 * n + m], c_recv.at[4 * n + m])
    for copy in started:
        copy.wait_send()


def gather_table(phase, mass, target_slot, target_star):
    hbm = pl.BlockSpec(memory_space=pltpu.HBM)
    vmem = pl.BlockSpec(memory_space=pltpu.VMEM)
    return pl.pallas_call(
        gather_kernel,
        out_shape=(
            jax.ShapeDtypeStruct((2, 4, 4, NZ, 4, 8, 128), F32),
            jax.ShapeDtypeStruct((2, PAIRS, 128), F32),
            jax.ShapeDtypeStruct((8, 128), jnp.int32),
        ),
        in_specs=[hbm] * 4,
        out_specs=(vmem,) * 3,
        scratch_shapes=[
            pltpu.VMEM((6, STAR_DEV), F32),
            pltpu.VMEM((1, STAR_DEV), F32),
            pltpu.VMEM((NBR + 1, ACT_DEV), jnp.int32),
            pltpu.VMEM((NBR + 1, ACT_DEV), jnp.int32),
            pltpu.VMEM((56, 128), jnp.int32),
            pltpu.VMEM((56, 128), jnp.int32),
            pltpu.VMEM((56, 128), jnp.int32),
            pltpu.SemaphoreType.DMA((4,)),
            pltpu.SemaphoreType.DMA((8,)),
            pltpu.SemaphoreType.DMA((8,)),
            pltpu.SemaphoreType.DMA((4,)),
            pltpu.SemaphoreType.DMA((4,)),
            pltpu.SemaphoreType.DMA((4, 4)),
            pltpu.SemaphoreType.DMA((4, 4)),
            pltpu.SemaphoreType.DMA((16,)),
            pltpu.SemaphoreType.DMA((16,)),
        ],
        compiler_params=pltpu.CompilerParams(
            collective_id=0, has_side_effects=True, vmem_limit_bytes=24 * 2**20
        ),
        name="gather_table",
    )(phase, mass, target_slot, target_star)


def split2(v):
    high = v.astype(BF16)
    return high, (v - high.astype(F32)).astype(BF16)


def split3_rows(v):
    high = v.astype(BF16).astype(F32)
    rest = v - high
    middle = rest.astype(BF16).astype(F32)
    return jnp.concatenate([high, middle, rest - middle], axis=0).astype(BF16)


def force_kernel(
    table_ref, req_ref, own_vec, old_ref, reg_ref, irr_ref, new_ref,
    own_smem, fetched, terms, moved, own_b, acc, copy_sem,
):
    fill = pltpu.make_async_copy(own_vec, own_smem, copy_sem)
    fill.start()
    fill.wait()
    lane8 = lax.broadcasted_iota(jnp.int32, (8, 128), 1)
    own = jnp.zeros((8, 128), F32)
    for i in range(ACT_DEV):
        code = own_smem[0, i]
        tile = table_ref[pl.ds(pl.multiple_of((code >> 7) * 8, 8), 8), :]
        turned = pltpu.roll(tile, (i + 128 - (code & 127)) & 127, 1)
        own = jnp.where(lane8 == i, turned, own)
    own_columns = jnp.transpose(own)
    for c in range(6):
        own_b[c] = jnp.broadcast_to(own_columns[0:ACT_DEV, c:c + 1], (ACT_DEV, 128))

    def fetch(pair, carry):
        first = jnp.broadcast_to(req_ref[0, pl.ds(pair, 1), :], (8, 128)).astype(jnp.int32)
        second = jnp.broadcast_to(req_ref[1, pl.ds(pair, 1), :], (8, 128)).astype(jnp.int32)
        index = first & 127
        quarter = second & 3
        both = []
        for h in range(2):
            got = None
            for t in range(4):
                tile = table_ref[pl.ds(pl.multiple_of(pair * 64 + h * 32 + t * 8, 8), 8), :]
                column = jnp.take_along_axis(tile, index, axis=1)
                got = column if t == 0 else jnp.where(quarter == t, column, got)
            both.append(got)
        fetched[pl.ds(pl.multiple_of(pair * 8, 8), 8), :] = jnp.where(lane8 < 64, both[0], both[1])
        return carry

    lax.fori_loop(0, PAIRS, fetch, 0, unroll=4)

    def neighbour_terms(g, carry):
        base = pl.multiple_of(g * 64, 64)
        lines = pl.ds(pl.multiple_of(g * 8, 8), 8)
        first = req_ref[0, lines, :]
        index = req_ref[1, lines, :].astype(jnp.int32) >> 2
        star_rows = [fetched[pl.ds(base + c, 8, stride=8), :] for c in range(7)]
        own_rows = [
            jnp.take_along_axis(jnp.broadcast_to(own[c:c + 1, :], (8, 128)), index, axis=1) for c in range(6)
        ]
        d = [star_rows[c] - own_rows[c] for c in range(3)]
        w = [star_rows[c] - own_rows[c] for c in range(3, 6)]
        q = SOFTEN + (d[0] * d[0] + d[1] * d[1] + d[2] * d[2])
        dw = d[0] * w[0] + d[1] * w[1] + d[2] * w[2]
        inverse = lax.rsqrt(q)
        square = inverse * inverse
        weight = jnp.where(first > 0.5, star_rows[6] * inverse * square, 0.0)
        radial = 3.0 * dw * square
        for c in range(3):
            terms[pl.ds(base + c, 8, stride=8), :] = weight * d[c]
            terms[pl.ds(base + 3 + c, 8, stride=8), :] = weight * (w[c] - radial * d[c])
        terms[pl.ds(base + 6, 8, stride=8), :] = jnp.zeros((8, 128), F32)
        terms[pl.ds(base + 7, 8, stride=8), :] = jnp.zeros((8, 128), F32)
        return carry

    lax.fori_loop(0, PAIRS // 8, neighbour_terms, 0)

    iota64 = lax.broadcasted_iota(jnp.int32, (ACT_DEV, 128), 0)

    def add_terms(p, carry):
        lefts, rights = [], []
        for k in range(8):
            pair = 8 * p + k
            t = terms[pl.ds(pl.multiple_of(pair * 8, 8), 8), :]
            high = t.astype(BF16).astype(F32)
            lefts.append(jnp.concatenate([high, t - high], axis=0).astype(BF16))
            index = req_ref[1, pl.ds(pair, 1), :].astype(jnp.int32) >> 2
            rights.append(jnp.where(iota64 == index, 1.0, 0.0).astype(BF16))
        return carry + lax.dot_general(
            jnp.concatenate(lefts, axis=1), jnp.concatenate(rights, axis=1), NT, preferred_element_type=F32
        )

    sums = lax.fori_loop(0, PAIRS // 8, add_terms, jnp.zeros((16, ACT_DEV), F32))
    irregular = (sums[0:6, :] + sums[8:14, :]) / NBR

    centre = jnp.sum(own[:, 0:ACT_DEV], axis=1, keepdims=True) * (1.0 / ACT_DEV)
    home = own - centre
    for c in range(6):
        own_b[c] = own_b[c] - jnp.broadcast_to(centre[c:c + 1, :], (ACT_DEV, 128))

    def shift(g, carry):
        base = pl.multiple_of(g * 64, 64)
        rows = [table_ref[pl.ds(base + c, 8, stride=8), :] - centre[c:c + 1, :] for c in range(6)]
        for c in range(6):
            moved[pl.ds(base + c, 8, stride=8), :] = rows[c]
        moved[pl.ds(base + 6, 8, stride=8), :] = jnp.zeros((8, 128), F32)
        moved[pl.ds(base + 7, 8, stride=8), :] = jnp.ones((8, 128), F32)
        return carry

    lax.fori_loop(0, OWNERS // 2, shift, 0, unroll=2)
    acc[...] = jnp.zeros_like(acc)

    def add_shards(g, carry):
        for u in range(UNROLL):
            shard = g * UNROLL + u
            base = pl.multiple_of(shard * 32, 32)
            tiles = [pl.multiple_of(base + 8 * t, 8) for t in range(4)]
            whole = jnp.concatenate([moved[pl.ds(tile, 8), :] for tile in tiles], axis=1)
            mass = jnp.concatenate([table_ref[pl.ds(tile + 6, 1), :] for tile in tiles], axis=1)
            emit = split3_rows(whole * mass)
            quarters = []
            for t in range(4):
                d = [moved[pl.ds(tiles[t] + c, 1), :] - own_b[c] for c in range(3)]
                w = [moved[pl.ds(tiles[t] + c, 1), :] - own_b[c] for c in range(3, 6)]
                q = (d[0] * d[0] + d[1] * d[1]) + (d[2] * d[2] + SOFTEN)
                inverse = lax.rsqrt(q)
                square = inverse * inverse
                v = square * inverse
                u_ = (d[0] * w[0] + d[1] * w[1] + d[2] * w[2]) * (v * square)
                quarters.append(split2(v) + split2(u_))
            weights = jnp.concatenate(
                [jnp.concatenate([part[k] for part in quarters], axis=1) for k in range(4)], axis=0
            )
            acc[...] += lax.dot_general(emit, weights, NT, preferred_element_type=F32)
        return carry

    lax.fori_loop(0, OWNERS // UNROLL, add_shards, 0)
    total = acc[...]
    total = total[0:8] + total[8:16] + total[16:24]
    v_rows = total[:, 0:64] + total[:, 64:128]
    u_rows = total[:, 128:192] + total[:, 192:256]
    home = home[:, 0:ACT_DEV]
    v_terms = v_rows - home * v_rows[7:8]
    u_terms = u_rows - home * u_rows[7:8]
    accel = v_terms[0:3] / STARS
    jerk = (v_terms[3:6] - 3.0 * u_terms[0:3]) / STARS

    old = old_ref[...]
    accel_new = accel + irregular[0:3]
    jerk_new = jerk + irregular[3:6]
    difference = old[0:3] - accel_new
    snap = -6.0 * difference - STEP * (4.0 * old[3:6] + 2.0 * jerk_new)
    crackle = 12.0 * difference + 6.0 * STEP * (old[3:6] + jerk_new)
    reg_ref[0:3, :] = accel
    reg_ref[3:6, :] = jerk
    irr_ref[...] = irregular
    new_ref[0:3, :] = own[0:3, 0:ACT_DEV] + STEP * STEP / 24.0 * snap + STEP * STEP / 120.0 * crackle
    new_ref[3:6, :] = own[3:6, 0:ACT_DEV] + STEP / 6.0 * snap + STEP / 24.0 * crackle


def forces(table, requests, own_codes, old_force):
    vmem = pl.BlockSpec(memory_space=pltpu.VMEM)
    out = jax.ShapeDtypeStruct((6, ACT_DEV), F32)
    return pl.pallas_call(
        force_kernel,
        out_shape=(out, out, out),
        in_specs=[vmem] * 4,
        out_specs=(vmem,) * 3,
        scratch_shapes=[
            pltpu.SMEM((8, 128), jnp.int32),
            pltpu.VMEM((PAIRS * 8, 128), F32),
            pltpu.VMEM((PAIRS * 8, 128), F32),
            pltpu.VMEM((OWNERS * 32, 128), F32),
            pltpu.VMEM((6, ACT_DEV, 128), F32),
            pltpu.VMEM((24, 256), F32),
            pltpu.SemaphoreType.DMA,
        ],
        compiler_params=pltpu.CompilerParams(vmem_limit_bytes=32 * 2**20),
        name="forces",
    )(table, requests, own_codes, old_force)


def per_device(field_phase, field_mass, old_force, target_slot, target_star):
    table, requests, own_codes = gather_table(
        field_phase, field_mass.reshape(1, STAR_DEV), target_slot, target_star
    )
    return forces(table.reshape(OWNERS * 32, 128), requests, own_codes, old_force)


def solution(mesh):
    split = P(None, ("grp", "blk"))
    return jax.shard_map(
        per_device,
        mesh=mesh,
        in_specs=(split, P(("grp", "blk")), split, split, split),
        out_specs=(split, split, split),
        check_vma=False,
    )
```

time: 105 us -> 89.3 us (0.85)
  Pallas kernels: 101 us -> 84.5 us
    pallas_call x1, Pallas kernels: 65.2 us -> 49.1 us  [forces(): pl.pallas_call(force_kernel, out_shape=(out, out, out), in_specs=[vmem] *...]
where the time goes in v2:
time: 89.3 us; the launch traced here: 89 us
  Pallas kernels  84.5 us (95%)
  local copies, waits for them, and re-layouts  3.8 us (4%)
    pallas_call x1, Pallas kernels, forces(): pl.pallas_call(force_kernel, out_shape=(out, out, out), in_specs=[vmem] *...  49.1 us
    pallas_call x1, Pallas kernels, gather_table(): pl.pallas_call(gather_kernel, out_shape=(jax.ShapeDtypeStruct((2, 4, 4, N...  35.4 us
    unnamed x8, local copies, waits for them, and re-layouts  3.8 us

profile of v2, /device:TPU:1, one launch (start us, length us, event | category | flops | bytes accessed | tf_op | source)
XLA Modules:
  0.0 89.0 jit_solution(12442902766149057441)
XLA Ops:
  0.6 0.9 copy.8.slot_hbm
  1.5 0.9 copy.9.star_hbm
  2.3 0.0 copy-start
  2.4 0.7 copy-done
  3.1 0.0 copy-start.2
  3.1 0.7 copy-done.2
  3.8 35.4 %gather_table.1 = (f32[2,4,4,8,4,8,128]{6,5,4,3,2,1,0:T(8,128)S(1)}, f32[2,128,128]{2,1,0:T(8,128)S(1)}, s32[8,128]{1,0:T(8,128)S(1)}) custom-call(f32[6,512]{1,0:T(8,128)S(1)} %copy-done, f32[1,512]{1,0:T(1,128)S(1)} %bitcast.3, s32[101,64]{1,0:T(8,128)S(1)} %copy.8.slot_hbm, s32[101,64]{1,0:T(8,128)S(1)} %copy.9.star_hbm), custom_call_target="tpu_custom_call" | custom-call | tf_op jit(solution)/shard_map/gather_table/pallas_call | solution.py:226
  39.2 0.0 copy-start.1
  39.2 0.7 copy-done.1
  39.9 49.1 %forces.1 = (f32[6,64]{1,0:T(8,128)}, f32[6,64]{1,0:T(8,128)}, f32[6,64]{1,0:T(8,128)}) custom-call(f32[8192,128]{1,0:T(8,128)S(1)} %bitcast.2, f32[2,128,128]{2,1,0:T(8,128)S(1)} %get-tuple-element.7.req_ref, s32[8,128]{1,0:T(8,128)S(1)} %get-tuple-element.8.own_vec, f32[6,64]{1,0:T(8,128)S(1)} %copy-done.1), custom_call_target="tpu_custom_call" | custom-call | tf_op jit(solution)/shard_map/forces/pallas_call | solution.py:420
Async XLA Ops:
  2.3 0.7 copy-start
  3.1 0.7 copy-start.2
  39.2 0.7 copy-start.1

commit v3 on v2

--- a/solution.py
+++ b/solution.py
@@ -22,8 +22,8 @@
 OWNERS = 256
 STARS = OWNERS * STAR_DEV
 PAIRS = OWNERS // 2
-HALF_ROWS = 51
 UNROLL = 8
+STRAIGHT = 3
 
 
 def table_place(owner):
@@ -36,26 +36,21 @@
 
 
 def build_requests(slot_ref, star_ref, req_ref, own_ref, place_scr, code_scr, column_scr):
-    lane = lax.broadcasted_iota(jnp.int32, (56, 128), 1)
-    row = lax.broadcasted_iota(jnp.int32, (56, 128), 0)
+    lane = lax.broadcasted_iota(jnp.int32, (ACT_DEV, 128), 1)
+    active = lax.broadcasted_iota(jnp.int32, (ACT_DEV, 128), 0)
     place_scr[...] = jnp.zeros_like(place_scr)
     code_scr[...] = jnp.zeros_like(code_scr)
-    place_scr[0:HALF_ROWS, 0:ACT_DEV] = slot_ref[0:HALF_ROWS, :]
-    place_scr[0:NBR + 1 - HALF_ROWS, ACT_DEV:128] = slot_ref[HALF_ROWS:NBR + 1, :]
-    code_scr[0:HALF_ROWS, 0:ACT_DEV] = star_ref[0:HALF_ROWS, :]
-    code_scr[0:NBR + 1 - HALF_ROWS, ACT_DEV:128] = star_ref[HALF_ROWS:NBR + 1, :]
+    place_scr[:, 0:NBR + 1] = slot_ref[...]
+    code_scr[:, 0:NBR + 1] = star_ref[...]
     slot = place_scr[...]
     star = code_scr[...]
     owner = (slot * 20165) >> 20
     within = slot - owner * MOST
     place = table_place(owner)
-    active = lane & 63
-    listed = (row < NBR + 1 - HALF_ROWS) | ((row == NBR + 1 - HALF_ROWS) & (lane < ACT_DEV))
-    neighbour = listed & ((row > 0) | (lane >= ACT_DEV))
-    place_scr[...] = jnp.where(neighbour, place >> 1, -1)
+    place_scr[...] = jnp.where((lane > 0) & (lane <= NBR), place >> 1, -1)
     column_scr[...] = within + 64 * (place & 1)
     code_scr[...] = star + active * 512
-    own_ref[...] = jnp.broadcast_to(place[0:1, :] * 512 + star[0:1, :], (8, 128))
+    own_ref[...] = place * 512 + star
 
     iota128 = lax.broadcasted_iota(jnp.int32, (128, 128), 0)
     req_ref[...] = jnp.zeros_like(req_ref)
@@ -81,11 +76,11 @@
         req_ref[1] += placed[:, 128:256]
         return carry
 
-    lax.fori_loop(0, 7, add_requests, 0)
+    lax.fori_loop(0, ACT_DEV // 8, add_requests, 0)
 
 
 def gather_kernel(
-    phase_hbm, mass_hbm, slot_hbm, star_hbm, out_ref, req_ref, own_ref,
+    phase_hbm, mass_hbm, slot_hbm, star_hbm, out_ref, req_ref, own_ref, fetched,
     phase_ref, mass_ref, slot_ref, star_ref, place_scr, code_scr, column_scr,
     in_sem, z_send, z_recv, a_send, a_recv, b_send, b_recv, c_send, c_recv,
 ):
@@ -118,6 +113,8 @@
     partners += [device(z, a_up, b, core), device(z, a_down, b, core)]
     partners += [device(z, a, b_up, core), device(z, a, b_down, core)]
     partners += [device(z, a, b, 1 - core), device(z, (a + 2) % 4, b, core)]
+    if STRAIGHT < 4:
+        partners += [device(z, a, (b + 2) % 4, core)]
 
     loads[0].wait()
     loads[1].wait()
@@ -134,6 +131,7 @@
     pl.semaphore_wait(barrier, len(partners))
 
     started = []
+    late = []
 
     def send(part, send_sem, recv_sem, target):
         copy = pltpu.make_async_remote_copy(
@@ -143,6 +141,8 @@
         started.append(copy)
 
     def await_recv(part, send_sem, recv_sem):
+        while late:
+            fetch(*late.pop())
         pltpu.make_async_remote_copy(
             src_ref=part, dst_ref=part, send_sem=send_sem, recv_sem=recv_sem,
             device_id=partners[11], device_id_type=MESH,
@@ -153,6 +153,27 @@
 
     def part(bb, aa, half):
         return out_ref.at[core, bb, aa, pl.ds(4 * half, 4)]
+
+    lane8 = lax.broadcasted_iota(jnp.int32, (8, 128), 1)
+
+    def fetch(cc, bb, aa):
+        def one_pair(k, carry):
+            pair = cc * 64 + (bb * 4 + aa) * 4 + k
+            first = jnp.broadcast_to(req_ref[0, pl.ds(pair, 1), :], (8, 128)).astype(jnp.int32)
+            second = jnp.broadcast_to(req_ref[1, pl.ds(pair, 1), :], (8, 128)).astype(jnp.int32)
+            index = first & 127
+            quarter = second & 3
+            both = []
+            for h in range(2):
+                got = None
+                for t in range(4):
+                    column = jnp.take_along_axis(out_ref[cc, bb, aa, 2 * k + h, t], index, axis=1)
+                    got = column if t == 0 else jnp.where(quarter == t, column, got)
+                both.append(got)
+            fetched[pl.ds(pl.multiple_of(pair * 8, 8), 8), :] = jnp.where(lane8 < 64, both[0], both[1])
+            return carry
+
+        lax.fori_loop(0, 4, one_pair, 0, unroll=True)
 
     for k in range(1, NZ):
         send(out_ref.at[core, b, a, z], z_send.at[k], z_recv.at[k], partners[k - 1])
@@ -168,23 +189,31 @@
 
     def send_core(bb, aa, n):
         send(block(bb, aa), c_send.at[n], c_recv.at[n], other)
+        late.append((core, bb, aa))
 
     def send_b(aa, n):
         send(block(b, aa), b_send.at[n, 0], b_recv.at[n, 0], to_b_up)
         send(block(b, aa), b_send.at[n, 1], b_recv.at[n, 1], to_b_down)
+        if n >= STRAIGHT:
+            send(block(b, aa), b_send.at[n, 2], b_recv.at[n, 2], partners[13])
 
     def near_b(aa, n):
         await_recv(block(b_down, aa), b_send.at[n, 0], b_recv.at[n, 0])
-        send(part(b_down, aa, 0), b_send.at[n, 2], b_recv.at[n, 2], to_b_up)
+        if n < STRAIGHT:
+            send(part(b_down, aa, 0), b_send.at[n, 2], b_recv.at[n, 2], to_b_up)
         send_core(b_down, aa, 4 * n + 1)
         await_recv(block(b_up, aa), b_send.at[n, 1], b_recv.at[n, 1])
-        send(part(b_up, aa, 1), b_send.at[n, 3], b_recv.at[n, 3], to_b_down)
+        if n < STRAIGHT:
+            send(part(b_up, aa, 1), b_send.at[n, 3], b_recv.at[n, 3], to_b_down)
         send_core(b_up, aa, 4 * n + 2)
 
     def far_b(aa, n):
         far = (b + 2) % 4
-        await_recv(part(far, aa, 0), b_send.at[n, 2], b_recv.at[n, 2])
-        await_recv(part(far, aa, 1), b_send.at[n, 3], b_recv.at[n, 3])
+        if n < STRAIGHT:
+            await_recv(part(far, aa, 0), b_send.at[n, 2], b_recv.at[n, 2])
+            await_recv(part(far, aa, 1), b_send.at[n, 3], b_recv.at[n, 3])
+        else:
+            await_recv(block(far, aa), b_send.at[n, 2], b_recv.at[n, 2])
         send_core(far, aa, 4 * n + 3)
 
     send(block(b, a), a_send.at[0], a_recv.at[0], to_a_up)
@@ -215,7 +244,9 @@
     oa, ob = b, a
     for n, da in enumerate((0, 3, 1, 2)):
         for m, db in enumerate((0, 3, 1, 2)):
-            await_recv(out_ref.at[1 - core, (ob + db) % 4, (oa + da) % 4], c_send.at[4 * n + m], c_recv.at[4 * n + m])
+            bb, aa = (ob + db) % 4, (oa + da) % 4
+            await_recv(out_ref.at[1 - core, bb, aa], c_send.at[4 * n + m], c_recv.at[4 * n + m])
+            fetch(1 - core, bb, aa)
     for copy in started:
         copy.wait_send()
 
@@ -228,18 +259,19 @@
         out_shape=(
             jax.ShapeDtypeStruct((2, 4, 4, NZ, 4, 8, 128), F32),
             jax.ShapeDtypeStruct((2, PAIRS, 128), F32),
-            jax.ShapeDtypeStruct((8, 128), jnp.int32),
+            jax.ShapeDtypeStruct((ACT_DEV, 128), jnp.int32),
+            jax.ShapeDtypeStruct((PAIRS * 8, 128), F32),
         ),
         in_specs=[hbm] * 4,
-        out_specs=(vmem,) * 3,
+        out_specs=(vmem,) * 4,
         scratch_shapes=[
             pltpu.VMEM((6, STAR_DEV), F32),
             pltpu.VMEM((1, STAR_DEV), F32),
-            pltpu.VMEM((NBR + 1, ACT_DEV), jnp.int32),
-            pltpu.VMEM((NBR + 1, ACT_DEV), jnp.int32),
-            pltpu.VMEM((56, 128), jnp.int32),
-            pltpu.VMEM((56, 128), jnp.int32),
-            pltpu.VMEM((56, 128), jnp.int32),
+            pltpu.VMEM((ACT_DEV, NBR + 1), jnp.int32),
+            pltpu.VMEM((ACT_DEV, NBR + 1), jnp.int32),
+            pltpu.VMEM((ACT_DEV, 128), jnp.int32),
+            pltpu.VMEM((ACT_DEV, 128), jnp.int32),
+            pltpu.VMEM((ACT_DEV, 128), jnp.int32),
             pltpu.SemaphoreType.DMA((4,)),
             pltpu.SemaphoreType.DMA((8,)),
             pltpu.SemaphoreType.DMA((8,)),
@@ -270,8 +302,8 @@
 
 
 def force_kernel(
-    table_ref, req_ref, own_vec, old_ref, reg_ref, irr_ref, new_ref,
-    own_smem, fetched, terms, moved, own_b, acc, copy_sem,
+    table_ref, req_ref, own_vec, fetched, old_ref, reg_ref, irr_ref, new_ref,
+    own_smem, terms, moved, own_b, acc, copy_sem,
 ):
     fill = pltpu.make_async_copy(own_vec, own_smem, copy_sem)
     fill.start()
@@ -279,31 +311,13 @@
     lane8 = lax.broadcasted_iota(jnp.int32, (8, 128), 1)
     own = jnp.zeros((8, 128), F32)
     for i in range(ACT_DEV):
-        code = own_smem[0, i]
+        code = own_smem[i, 0]
         tile = table_ref[pl.ds(pl.multiple_of((code >> 7) * 8, 8), 8), :]
         turned = pltpu.roll(tile, (i + 128 - (code & 127)) & 127, 1)
         own = jnp.where(lane8 == i, turned, own)
     own_columns = jnp.transpose(own)
     for c in range(6):
         own_b[c] = jnp.broadcast_to(own_columns[0:ACT_DEV, c:c + 1], (ACT_DEV, 128))
-
-    def fetch(pair, carry):
-        first = jnp.broadcast_to(req_ref[0, pl.ds(pair, 1), :], (8, 128)).astype(jnp.int32)
-        second = jnp.broadcast_to(req_ref[1, pl.ds(pair, 1), :], (8, 128)).astype(jnp.int32)
-        index = first & 127
-        quarter = second & 3
-        both = []
-        for h in range(2):
-            got = None
-            for t in range(4):
-                tile = table_ref[pl.ds(pl.multiple_of(pair * 64 + h * 32 + t * 8, 8), 8), :]
-                column = jnp.take_along_axis(tile, index, axis=1)
-                got = column if t == 0 else jnp.where(quarter == t, column, got)
-            both.append(got)
-        fetched[pl.ds(pl.multiple_of(pair * 8, 8), 8), :] = jnp.where(lane8 < 64, both[0], both[1])
-        return carry
-
-    lax.fori_loop(0, PAIRS, fetch, 0, unroll=4)
 
     def neighbour_terms(g, carry):
         base = pl.multiple_of(g * 64, 64)
@@ -414,17 +428,16 @@
     new_ref[3:6, :] = own[3:6, 0:ACT_DEV] + STEP / 6.0 * snap + STEP / 24.0 * crackle
 
 
-def forces(table, requests, own_codes, old_force):
+def forces(table, requests, own_codes, fetched, old_force):
     vmem = pl.BlockSpec(memory_space=pltpu.VMEM)
     out = jax.ShapeDtypeStruct((6, ACT_DEV), F32)
     return pl.pallas_call(
         force_kernel,
         out_shape=(out, out, out),
-        in_specs=[vmem] * 4,
+        in_specs=[vmem] * 5,
         out_specs=(vmem,) * 3,
         scratch_shapes=[
-            pltpu.SMEM((8, 128), jnp.int32),
-            pltpu.VMEM((PAIRS * 8, 128), F32),
+            pltpu.SMEM((ACT_DEV, 128), jnp.int32),
             pltpu.VMEM((PAIRS * 8, 128), F32),
             pltpu.VMEM((OWNERS * 32, 128), F32),
             pltpu.VMEM((6, ACT_DEV, 128), F32),
@@ -433,14 +446,14 @@
         ],
         compiler_params=pltpu.CompilerParams(vmem_limit_bytes=32 * 2**20),
         name="forces",
-    )(table, requests, own_codes, old_force)
+    )(table, requests, own_codes, fetched, old_force)
 
 
 def per_device(field_phase, field_mass, old_force, target_slot, target_star):
-    table, requests, own_codes = gather_table(
-        field_phase, field_mass.reshape(1, STAR_DEV), target_slot, target_star
+    table, requests, own_codes, fetched = gather_table(
+        field_phase, field_mass.reshape(1, STAR_DEV), target_slot.T, target_star.T
     )
-    return forces(table.reshape(OWNERS * 32, 128), requests, own_codes, old_force)
+    return forces(table.reshape(OWNERS * 32, 128), requests, own_codes, fetched, old_force)
 
 
 def solution(mesh):

time: 89.3 us -> 84.6 us (0.947)
  Pallas kernels: 84.5 us -> 80 us
    pallas_call x1, Pallas kernels: 49.1 us -> 45.3 us  [forces(): pl.pallas_call(force_kernel, out_shape=(out, out, out), in_specs=[vmem] *...]
    unnamed x8 -> x10, local copies, waits for them, and re-layouts: 3.8 us -> 3.59 us
where the time goes in v3:
time: 84.6 us; the launch traced here: 84.3 us
  Pallas kernels  80 us (95%)
  local copies, waits for them, and re-layouts  3.59 us (4%)
    pallas_call x1, Pallas kernels, forces(): pl.pallas_call(force_kernel, out_shape=(out, out, out), in_specs=[vmem] *...  45.3 us
    pallas_call x1, Pallas kernels, gather_table(): pl.pallas_call(gather_kernel, out_shape=(jax.ShapeDtypeStruct((2, 4, 4, N...  34.7 us
    unnamed x10, local copies, waits for them, and re-layouts  3.59 us

profile of v3, /device:TPU:1, one launch (start us, length us, event | category | flops | bytes accessed | tf_op | source)
XLA Modules:
  0.0 84.3 jit_solution(9374932175223729035)
XLA Ops:
  0.6 0.0 copy-start
  0.6 0.7 copy-done
  1.4 0.0 copy-start.1
  1.4 0.8 copy-done.1
  2.1 0.0 copy-start.2
  2.2 0.7 copy-done.2
  2.9 0.0 copy-start.4
  2.9 0.7 copy-done.4
  3.5 34.7 %gather_table.1 = (f32[2,4,4,8,4,8,128]{6,5,4,3,2,1,0:T(8,128)S(1)}, f32[2,128,128]{2,1,0:T(8,128)S(1)}, s32[64,128]{1,0:T(8,128)S(1)}, f32[1024,128]{1,0:T(8,128)S(1)}) custom-call(f32[6,512]{1,0:T(8,128)S(1)} %copy-done.2, f32[1,512]{1,0:T(1,128)S(1)} %bitcast.7, s32[64,101]{1,0:T(8,128)S(1)} %bitcast.5, s32[64,101]{1,0:T(8,128)S(1)} %bitcast.6), custom_call_target="tpu_custom_call" | custom-call | tf_op jit(solution)/shard_map/gather_table/pallas_call | solution.py:257
  38.2 0.0 copy-start.3
  38.3 0.7 copy-done.3
  38.9 45.3 %forces.1 = (f32[6,64]{1,0:T(8,128)}, f32[6,64]{1,0:T(8,128)}, f32[6,64]{1,0:T(8,128)}) custom-call(f32[8192,128]{1,0:T(8,128)S(1)} %bitcast.4, f32[2,128,128]{2,1,0:T(8,128)S(1)} %get-tuple-element.8.req_ref, s32[64,128]{1,0:T(8,128)S(1)} %get-tuple-element.9.own_vec, f32[1024,128]{1,0:T(8,128)S(1)} %get-tuple-element.10.fetched, f32[6,64]{1,0:T(8,128)S(1)} %copy-done.3), custom_call_target="tpu_custom_call" | custom-call | tf_op jit(solution)/shard_map/forces/pallas_call | solution.py:434
Async XLA Ops:
  0.6 0.8 copy-start
  1.4 0.8 copy-start.1
  2.1 0.7 copy-start.2
  2.9 0.7 copy-start.4
  38.2 0.7 copy-start.3

commit v4 on v3

--- a/solution.py
+++ b/solution.py
@@ -22,7 +22,8 @@
 OWNERS = 256
 STARS = OWNERS * STAR_DEV
 PAIRS = OWNERS // 2
-UNROLL = 8
+UNROLL = 32
+ON_MATRIX = (0, 4, 8, 12, 16, 20, 24, 28)
 STRAIGHT = 3
 
 
@@ -303,7 +304,7 @@
 
 def force_kernel(
     table_ref, req_ref, own_vec, fetched, old_ref, reg_ref, irr_ref, new_ref,
-    own_smem, terms, moved, own_b, acc, copy_sem,
+    own_smem, terms, moved, left_scr, own_b, acc, copy_sem,
 ):
     fill = pltpu.make_async_copy(own_vec, own_smem, copy_sem)
     fill.start()
@@ -319,7 +320,7 @@
     for c in range(6):
         own_b[c] = jnp.broadcast_to(own_columns[0:ACT_DEV, c:c + 1], (ACT_DEV, 128))
 
-    def neighbour_terms(g, carry):
+    def neighbour_terms(g):
         base = pl.multiple_of(g * 64, 64)
         lines = pl.ds(pl.multiple_of(g * 8, 8), 8)
         first = req_ref[0, lines, :]
@@ -341,9 +342,6 @@
             terms[pl.ds(base + 3 + c, 8, stride=8), :] = weight * (w[c] - radial * d[c])
         terms[pl.ds(base + 6, 8, stride=8), :] = jnp.zeros((8, 128), F32)
         terms[pl.ds(base + 7, 8, stride=8), :] = jnp.zeros((8, 128), F32)
-        return carry
-
-    lax.fori_loop(0, PAIRS // 8, neighbour_terms, 0)
 
     iota64 = lax.broadcasted_iota(jnp.int32, (ACT_DEV, 128), 0)
 
@@ -360,9 +358,6 @@
             jnp.concatenate(lefts, axis=1), jnp.concatenate(rights, axis=1), NT, preferred_element_type=F32
         )
 
-    sums = lax.fori_loop(0, PAIRS // 8, add_terms, jnp.zeros((16, ACT_DEV), F32))
-    irregular = (sums[0:6, :] + sums[8:14, :]) / NBR
-
     centre = jnp.sum(own[:, 0:ACT_DEV], axis=1, keepdims=True) * (1.0 / ACT_DEV)
     home = own - centre
     for c in range(6):
@@ -373,38 +368,80 @@
         rows = [table_ref[pl.ds(base + c, 8, stride=8), :] - centre[c:c + 1, :] for c in range(6)]
         for c in range(6):
             moved[pl.ds(base + c, 8, stride=8), :] = rows[c]
-        moved[pl.ds(base + 6, 8, stride=8), :] = jnp.zeros((8, 128), F32)
+        moved[pl.ds(base + 6, 8, stride=8), :] = rows[0] * rows[3] + rows[1] * rows[4] + rows[2] * rows[5]
         moved[pl.ds(base + 7, 8, stride=8), :] = jnp.ones((8, 128), F32)
         return carry
 
     lax.fori_loop(0, OWNERS // 2, shift, 0, unroll=2)
+    s_own = jnp.sum(home[0:3, :] * home[3:6, :], axis=0, keepdims=True)
+    left = jnp.concatenate([-home[3:6, :], -home[0:3, :], jnp.ones((1, 128), F32), s_own], axis=0)
+    left_h = left.astype(BF16).astype(F32)
+    left_m = (left - left_h).astype(BF16).astype(F32)
+    left_l = left - left_h - left_m
+    left = jnp.concatenate([left_h, left_h, left_m, left_m, left_h, left_l, jnp.zeros((80, 128), F32)], axis=0)
+    left = jnp.transpose(left)[0:ACT_DEV, 0:64]
+    none = jnp.zeros((ACT_DEV, 64), F32)
+    for n in range(4):
+        line = jnp.concatenate([left if k == n else none for k in range(4)], axis=1)
+        left_scr[n * 64:n * 64 + 64, :] = line.astype(BF16)
+    blank = jnp.zeros((16, 256), BF16)
+
     acc[...] = jnp.zeros_like(acc)
 
-    def add_shards(g, carry):
+    def add_shards(g, sums):
+        for k in range(UNROLL // 16):
+            neighbour_terms(g * (UNROLL // 16) + k)
+            sums = add_terms(g * (UNROLL // 16) + k, sums)
+        wholes, products = [], []
         for u in range(UNROLL):
+            tiles = [pl.multiple_of((g * UNROLL + u) * 32 + 8 * t, 8) for t in range(4)]
+            wholes.append(jnp.concatenate([moved[pl.ds(tile, 8), :] for tile in tiles], axis=1))
+            products.append(None)
+        for first in ON_MATRIX:
+            stack = []
+            for u in (first, first + 1):
+                high = wholes[u].astype(BF16).astype(F32)
+                rest = wholes[u] - high
+                middle = rest.astype(BF16).astype(F32)
+                pair = jnp.concatenate([high, middle], axis=0).astype(BF16)
+                last = jnp.concatenate([rest - middle, high], axis=0).astype(BF16)
+                for lanes in (slice(0, 256), slice(256, 512)):
+                    stack += [pair[:, lanes], pair[:, lanes], last[:, lanes], blank]
+            product = jnp.dot(left_scr[...], jnp.concatenate(stack, axis=0), preferred_element_type=F32)
+            for k in range(2):
+                products[first + k] = jnp.concatenate(
+                    [product[128 * k:128 * k + 64], product[128 * k + 64:128 * k + 128]], axis=1
+                )
+        on = [first + k for first in ON_MATRIX for k in range(2)]
+        for u in [u for u in range(UNROLL) if u not in on] + on:
             shard = g * UNROLL + u
             base = pl.multiple_of(shard * 32, 32)
             tiles = [pl.multiple_of(base + 8 * t, 8) for t in range(4)]
-            whole = jnp.concatenate([moved[pl.ds(tile, 8), :] for tile in tiles], axis=1)
+            whole = wholes[u]
             mass = jnp.concatenate([table_ref[pl.ds(tile + 6, 1), :] for tile in tiles], axis=1)
             emit = split3_rows(whole * mass)
             quarters = []
             for t in range(4):
                 d = [moved[pl.ds(tiles[t] + c, 1), :] - own_b[c] for c in range(3)]
-                w = [moved[pl.ds(tiles[t] + c, 1), :] - own_b[c] for c in range(3, 6)]
+                if products[u] is None:
+                    w = [moved[pl.ds(tiles[t] + c, 1), :] - own_b[c] for c in range(3, 6)]
+                    dw = d[0] * w[0] + d[1] * w[1] + d[2] * w[2]
+                else:
+                    dw = products[u][:, t * 128:t * 128 + 128]
                 q = (d[0] * d[0] + d[1] * d[1]) + (d[2] * d[2] + SOFTEN)
                 inverse = lax.rsqrt(q)
                 square = inverse * inverse
                 v = square * inverse
-                u_ = (d[0] * w[0] + d[1] * w[1] + d[2] * w[2]) * (v * square)
+                u_ = dw * (v * square)
                 quarters.append(split2(v) + split2(u_))
             weights = jnp.concatenate(
                 [jnp.concatenate([part[k] for part in quarters], axis=1) for k in range(4)], axis=0
             )
             acc[...] += lax.dot_general(emit, weights, NT, preferred_element_type=F32)
-        return carry
-
-    lax.fori_loop(0, OWNERS // UNROLL, add_shards, 0)
+        return sums
+
+    sums = lax.fori_loop(0, OWNERS // UNROLL, add_shards, jnp.zeros((16, ACT_DEV), F32))
+    irregular = (sums[0:6, :] + sums[8:14, :]) / NBR
     total = acc[...]
     total = total[0:8] + total[8:16] + total[16:24]
     v_rows = total[:, 0:64] + total[:, 64:128]
@@ -440,6 +477,7 @@
             pltpu.SMEM((ACT_DEV, 128), jnp.int32),
             pltpu.VMEM((PAIRS * 8, 128), F32),
             pltpu.VMEM((OWNERS * 32, 128), F32),
+            pltpu.VMEM((256, 256), BF16),
             pltpu.VMEM((6, ACT_DEV, 128), F32),
             pltpu.VMEM((24, 256), F32),
             pltpu.SemaphoreType.DMA,

time: 84.6 us -> 74.3 us (0.88)
  Pallas kernels: 80 us -> 69.7 us
    pallas_call x1, Pallas kernels: 45.3 us -> 35.1 us  [forces(): pl.pallas_call(force_kernel, out_shape=(out, out, out), in_specs=[vmem] *...]
where the time goes in v4:
time: 74.3 us; the launch traced here: 74 us
  Pallas kernels  69.7 us (94%)
  local copies, waits for them, and re-layouts  3.59 us (5%)
    pallas_call x1, Pallas kernels, forces(): pl.pallas_call(force_kernel, out_shape=(out, out, out), in_specs=[vmem] *...  35.1 us
    pallas_call x1, Pallas kernels, gather_table(): pl.pallas_call(gather_kernel, out_shape=(jax.ShapeDtypeStruct((2, 4, 4, N...  34.7 us
    unnamed x10, local copies, waits for them, and re-layouts  3.59 us

profile of v4, /device:TPU:1, one launch (start us, length us, event | category | flops | bytes accessed | tf_op | source)
XLA Modules:
  0.0 74.0 jit_solution(12863580986686749271)
XLA Ops:
  0.6 0.0 copy-start
  0.6 0.7 %copy-done = s32[101,64]{0,1:T(8,128)S(1)} copy-done((s32[101,64]{0,1:T(8,128)S(1)}, s32[101,64]{0,1:T(8,128)}, u32[]{:S(2)}) %copy-start) | copy-done | bytes 25880
  1.4 0.0 copy-start.1
  1.4 0.8 %copy-done.1 = s32[101,64]{0,1:T(8,128)S(1)} copy-done((s32[101,64]{0,1:T(8,128)S(1)}, s32[101,64]{0,1:T(8,128)}, u32[]{:S(2)}) %copy-start.1) | copy-done | bytes 25880
  2.1 0.0 copy-start.2
  2.2 0.7 copy-done.2
  2.9 0.0 copy-start.4
  2.9 0.7 copy-done.4
  3.5 34.7 %gather_table.1 = (f32[2,4,4,8,4,8,128]{6,5,4,3,2,1,0:T(8,128)S(1)}, f32[2,128,128]{2,1,0:T(8,128)S(1)}, s32[64,128]{1,0:T(8,128)S(1)}, f32[1024,128]{1,0:T(8,128)S(1)}) custom-call(f32[6,512]{1,0:T(8,128)S(1)} %copy-done.2, f32[1,512]{1,0:T(1,128)S(1)} %bitcast.7, s32[64,101]{1,0:T(8,128)S(1)} %bitcast.5, s32[64,101]{1,0:T(8,128)S(1)} %bitcast.6), custom_call_target="tpu_custom_call" | custom-call | tf_op jit(solution)/shard_map/gather_table/pallas_call | solution.py:258
  38.2 0.0 copy-start.3
  38.3 0.7 copy-done.3
  38.9 35.1 %forces.1 = (f32[6,64]{1,0:T(8,128)}, f32[6,64]{1,0:T(8,128)}, f32[6,64]{1,0:T(8,128)}) custom-call(f32[8192,128]{1,0:T(8,128)S(1)} %bitcast.4, f32[2,128,128]{2,1,0:T(8,128)S(1)} %get-tuple-element.8.req_ref, s32[64,128]{1,0:T(8,128)S(1)} %get-tuple-element.9.own_vec, f32[1024,128]{1,0:T(8,128)S(1)} %get-tuple-element.10.fetched, f32[6,64]{1,0:T(8,128)S(1)} %copy-done.3), custom_call_target="tpu_custom_call" | custom-call | tf_op jit(solution)/shard_map/forces/pallas_call | solution.py:471
Async XLA Ops:
  0.6 0.8 %copy-start = (s32[101,64]{0,1:T(8,128)S(1)}, s32[101,64]{0,1:T(8,128)}, u32[]{:S(2)}) copy-start(s32[101,64]{0,1:T(8,128)} %param.8) | copy-start | bytes 77572
  1.4 0.8 %copy-start.1 = (s32[101,64]{0,1:T(8,128)S(1)}, s32[101,64]{0,1:T(8,128)}, u32[]{:S(2)}) copy-start(s32[101,64]{0,1:T(8,128)} %param.9) | copy-start | bytes 77572
  2.1 0.7 copy-start.2
  2.9 0.7 copy-start.4
  38.2 0.7 copy-start.3

commit v5 on v4

--- a/solution.py
+++ b/solution.py
@@ -150,10 +150,10 @@
         ).wait_recv()
 
     def block(bb, aa):
-        return out_ref.at[core, bb, aa]
+        return out_ref.at[core, bb, aa, :, :, pl.ds(0, 7)]
 
     def part(bb, aa, half):
-        return out_ref.at[core, bb, aa, pl.ds(4 * half, 4)]
+        return out_ref.at[core, bb, aa, pl.ds(4 * half, 4), :, pl.ds(0, 7)]
 
     lane8 = lax.broadcasted_iota(jnp.int32, (8, 128), 1)
 
@@ -177,12 +177,9 @@
         lax.fori_loop(0, 4, one_pair, 0, unroll=True)
 
     for k in range(1, NZ):
-        send(out_ref.at[core, b, a, z], z_send.at[k], z_recv.at[k], partners[k - 1])
-    loads[2].wait()
-    loads[3].wait()
-    build_requests(slot_ref, star_ref, req_ref, own_ref, place_scr, code_scr, column_scr)
+        send(out_ref.at[core, b, a, z, :, pl.ds(0, 7)], z_send.at[k], z_recv.at[k], partners[k - 1])
     for k in range(1, NZ):
-        await_recv(out_ref.at[core, b, a, (z + NZ - k) % NZ], z_send.at[k], z_recv.at[k])
+        await_recv(out_ref.at[core, b, a, (z + NZ - k) % NZ, :, pl.ds(0, 7)], z_send.at[k], z_recv.at[k])
 
     to_a_up, to_a_down = partners[7], partners[8]
     to_b_up, to_b_down = partners[9], partners[10]
@@ -222,6 +219,9 @@
     send(block(b, a), a_send.at[2], a_recv.at[2], partners[12])
     send_b(a, 0)
     send_core(b, a, 0)
+    loads[2].wait()
+    loads[3].wait()
+    build_requests(slot_ref, star_ref, req_ref, own_ref, place_scr, code_scr, column_scr)
 
     await_recv(block(b, a_down), a_send.at[0], a_recv.at[0])
     send_b(a_down, 1)
@@ -246,7 +246,7 @@
     for n, da in enumerate((0, 3, 1, 2)):
         for m, db in enumerate((0, 3, 1, 2)):
             bb, aa = (ob + db) % 4, (oa + da) % 4
-            await_recv(out_ref.at[1 - core, bb, aa], c_send.at[4 * n + m], c_recv.at[4 * n + m])
+            await_recv(out_ref.at[1 - core, bb, aa, :, :, pl.ds(0, 7)], c_send.at[4 * n + m], c_recv.at[4 * n + m])
             fetch(1 - core, bb, aa)
     for copy in started:
         copy.wait_send()
@@ -303,9 +303,11 @@
 
 
 def force_kernel(
-    table_ref, req_ref, own_vec, fetched, old_ref, reg_ref, irr_ref, new_ref,
-    own_smem, terms, moved, left_scr, own_b, acc, copy_sem,
+    table_ref, req_ref, own_vec, fetched, old_hbm, reg_ref, irr_ref, new_ref,
+    own_smem, old_scr, terms, moved, left_scr, own_b, acc, copy_sem, old_sem,
 ):
+    load = pltpu.make_async_copy(old_hbm, old_scr, old_sem)
+    load.start()
     fill = pltpu.make_async_copy(own_vec, own_smem, copy_sem)
     fill.start()
     fill.wait()
@@ -452,7 +454,8 @@
     accel = v_terms[0:3] / STARS
     jerk = (v_terms[3:6] - 3.0 * u_terms[0:3]) / STARS
 
-    old = old_ref[...]
+    load.wait()
+    old = old_scr[...]
     accel_new = accel + irregular[0:3]
     jerk_new = jerk + irregular[3:6]
     difference = old[0:3] - accel_new
@@ -471,27 +474,33 @@
     return pl.pallas_call(
         force_kernel,
         out_shape=(out, out, out),
-        in_specs=[vmem] * 5,
+        in_specs=[vmem] * 4 + [pl.BlockSpec(memory_space=pltpu.HBM)],
         out_specs=(vmem,) * 3,
         scratch_shapes=[
             pltpu.SMEM((ACT_DEV, 128), jnp.int32),
+            pltpu.VMEM((6, ACT_DEV), F32),
             pltpu.VMEM((PAIRS * 8, 128), F32),
             pltpu.VMEM((OWNERS * 32, 128), F32),
             pltpu.VMEM((256, 256), BF16),
             pltpu.VMEM((6, ACT_DEV, 128), F32),
             pltpu.VMEM((24, 256), F32),
             pltpu.SemaphoreType.DMA,
+            pltpu.SemaphoreType.DMA,
         ],
         compiler_params=pltpu.CompilerParams(vmem_limit_bytes=32 * 2**20),
         name="forces",
     )(table, requests, own_codes, fetched, old_force)
 
 
+def in_hbm(array):
+    return pltpu.with_memory_space_constraint(array, pltpu.HBM)
+
+
 def per_device(field_phase, field_mass, old_force, target_slot, target_star):
     table, requests, own_codes, fetched = gather_table(
-        field_phase, field_mass.reshape(1, STAR_DEV), target_slot.T, target_star.T
+        in_hbm(field_phase), in_hbm(field_mass.reshape(1, STAR_DEV)), in_hbm(target_slot.T), in_hbm(target_star.T)
     )
-    return forces(table.reshape(OWNERS * 32, 128), requests, own_codes, fetched, old_force)
+    return forces(table.reshape(OWNERS * 32, 128), requests, own_codes, fetched, in_hbm(old_force))
 
 
 def solution(mesh):

time: 74.3 us -> 70.2 us (0.945)
  local copies, waits for them, and re-layouts: 3.59 us -> 0 us
    unnamed x10 -> x0, local copies, waits for them, and re-layouts: 3.59 us -> none
    pallas_call x1, Pallas kernels: 34.7 us -> 33.7 us  [gather_table(): pl.pallas_call(gather_kernel, out_shape=(jax.ShapeDtypeStruct((2, 4, 4, N...]
where the time goes in v5:
time: 70.2 us; the launch traced here: 70 us
  Pallas kernels  69.4 us (99%)
    pallas_call x1, Pallas kernels, forces(): pl.pallas_call(force_kernel, out_shape=(out, out, out), in_specs=[vmem] *...  35.7 us
    pallas_call x1, Pallas kernels, gather_table(): pl.pallas_call(gather_kernel, out_shape=(jax.ShapeDtypeStruct((2, 4, 4, N...  33.7 us

profile of v5, /device:TPU:1, one launch (start us, length us, event | category | flops | bytes accessed | tf_op | source)
XLA Modules:
  0.0 70.0 jit_solution(15042235535478006690)
XLA Ops:
  0.6 33.7 %gather_table.1 = (f32[2,4,4,8,4,8,128]{6,5,4,3,2,1,0:T(8,128)S(1)}, f32[2,128,128]{2,1,0:T(8,128)S(1)}, s32[64,128]{1,0:T(8,128)S(1)}, f32[1024,128]{1,0:T(8,128)S(1)}) custom-call(f32[6,512]{1,0:T(8,128)} %phase_hbm.1, f32[1,512]{1,0:T(1,128)} %bitcast.7, s32[64,101]{1,0:T(8,128)} %bitcast.5, s32[64,101]{1,0:T(8,128)} %bitcast.6), custom_call_target="tpu_custom_call" | custom-call | tf_op jit(solution)/shard_map/gather_table/pallas_call | solution.py:258
  34.3 35.7 %forces.1 = (f32[6,64]{1,0:T(8,128)}, f32[6,64]{1,0:T(8,128)}, f32[6,64]{1,0:T(8,128)}) custom-call(f32[8192,128]{1,0:T(8,128)S(1)} %bitcast.4, f32[2,128,128]{2,1,0:T(8,128)S(1)} %get-tuple-element.8.req_ref, s32[64,128]{1,0:T(8,128)S(1)} %get-tuple-element.9.own_vec, f32[1024,128]{1,0:T(8,128)S(1)} %get-tuple-element.10.fetched, f32[6,64]{1,0:T(8,128)} %old_hbm.1), custom_call_target="tpu_custom_call" | custom-call | tf_op jit(solution)/shard_map/forces/pallas_call | solution.py:474

commit v6 on v5

--- a/solution.py
+++ b/solution.py
@@ -117,6 +117,10 @@
     if STRAIGHT < 4:
         partners += [device(z, a, (b + 2) % 4, core)]
 
+    barrier = pltpu.get_barrier_semaphore()
+    for partner in partners:
+        pl.semaphore_signal(barrier, inc=1, device_id=partner, device_id_type=MESH)
+
     loads[0].wait()
     loads[1].wait()
 
@@ -126,9 +130,6 @@
         out_ref[core, b, a, z, t, 6:7, :] = mass_ref[:, lanes]
         out_ref[core, b, a, z, t, 7:8, :] = jnp.ones((1, 128), F32)
 
-    barrier = pltpu.get_barrier_semaphore()
-    for partner in partners:
-        pl.semaphore_signal(barrier, inc=1, device_id=partner, device_id_type=MESH)
     pl.semaphore_wait(barrier, len(partners))
 
     started = []
@@ -225,9 +226,9 @@
 
     await_recv(block(b, a_down), a_send.at[0], a_recv.at[0])
     send_b(a_down, 1)
-    send_core(b, a_down, 4)
     await_recv(block(b, a_up), a_send.at[1], a_recv.at[1])
     send_b(a_up, 2)
+    send_core(b, a_down, 4)
     send_core(b, a_up, 8)
     a_far = (a + 2) % 4
     near_b(a, 0)

time: 70.2 us -> 69.6 us (level)
  no operation moved by 1% of the time
where the time goes in v6:
time: 69.6 us; the launch traced here: 69.5 us
  Pallas kernels  68.8 us (99%)
    pallas_call x1, Pallas kernels, forces(): pl.pallas_call(force_kernel, out_shape=(out, out, out), in_specs=[vmem] *...  35.7 us
    pallas_call x1, Pallas kernels, gather_table(): pl.pallas_call(gather_kernel, out_shape=(jax.ShapeDtypeStruct((2, 4, 4, N...  33.1 us

profile of v6, /device:TPU:1, one launch (start us, length us, event | category | flops | bytes accessed | tf_op | source)
XLA Modules:
  0.0 69.5 jit_solution(7106261762622672926)
XLA Ops:
  0.6 33.1 %gather_table.1 = (f32[2,4,4,8,4,8,128]{6,5,4,3,2,1,0:T(8,128)S(1)}, f32[2,128,128]{2,1,0:T(8,128)S(1)}, s32[64,128]{1,0:T(8,128)S(1)}, f32[1024,128]{1,0:T(8,128)S(1)}) custom-call(f32[6,512]{1,0:T(8,128)} %phase_hbm.1, f32[1,512]{1,0:T(1,128)} %bitcast.7, s32[64,101]{1,0:T(8,128)} %bitcast.5, s32[64,101]{1,0:T(8,128)} %bitcast.6), custom_call_target="tpu_custom_call" | custom-call | tf_op jit(solution)/shard_map/gather_table/pallas_call | solution.py:259
  33.8 35.7 %forces.1 = (f32[6,64]{1,0:T(8,128)}, f32[6,64]{1,0:T(8,128)}, f32[6,64]{1,0:T(8,128)}) custom-call(f32[8192,128]{1,0:T(8,128)S(1)} %bitcast.4, f32[2,128,128]{2,1,0:T(8,128)S(1)} %get-tuple-element.8.req_ref, s32[64,128]{1,0:T(8,128)S(1)} %get-tuple-element.9.own_vec, f32[1024,128]{1,0:T(8,128)S(1)} %get-tuple-element.10.fetched, f32[6,64]{1,0:T(8,128)} %old_hbm.1), custom_call_target="tpu_custom_call" | custom-call | tf_op jit(solution)/shard_map/forces/pallas_call | solution.py:475

commit v7 on v6

--- a/solution.py
+++ b/solution.py
@@ -22,8 +22,8 @@
 OWNERS = 256
 STARS = OWNERS * STAR_DEV
 PAIRS = OWNERS // 2
-UNROLL = 32
-ON_MATRIX = (0, 4, 8, 12, 16, 20, 24, 28)
+UNROLL = 64
+ON_MATRIX = tuple(range(0, 64, 4))
 STRAIGHT = 3
 
 

time: 69.6 us -> 68.5 us (0.984)
  Pallas kernels: 68.8 us -> 67.7 us
    pallas_call x1, Pallas kernels: 35.7 us -> 34.6 us  [forces(): pl.pallas_call(force_kernel, out_shape=(out, out, out), in_specs=[vmem] *...]
where the time goes in v7:
time: 68.5 us; the launch traced here: 68.4 us
  Pallas kernels  67.7 us (99%)
    pallas_call x1, Pallas kernels, forces(): pl.pallas_call(force_kernel, out_shape=(out, out, out), in_specs=[vmem] *...  34.6 us
    pallas_call x1, Pallas kernels, gather_table(): pl.pallas_call(gather_kernel, out_shape=(jax.ShapeDtypeStruct((2, 4, 4, N...  33.1 us

profile of v7, /device:TPU:1, one launch (start us, length us, event | category | flops | bytes accessed | tf_op | source)
XLA Modules:
  0.0 68.4 jit_solution(2891744925392617531)
XLA Ops:
  0.6 33.1 %gather_table.1 = (f32[2,4,4,8,4,8,128]{6,5,4,3,2,1,0:T(8,128)S(1)}, f32[2,128,128]{2,1,0:T(8,128)S(1)}, s32[64,128]{1,0:T(8,128)S(1)}, f32[1024,128]{1,0:T(8,128)S(1)}) custom-call(f32[6,512]{1,0:T(8,128)} %phase_hbm.1, f32[1,512]{1,0:T(1,128)} %bitcast.7, s32[64,101]{1,0:T(8,128)} %bitcast.5, s32[64,101]{1,0:T(8,128)} %bitcast.6), custom_call_target="tpu_custom_call" | custom-call | tf_op jit(solution)/shard_map/gather_table/pallas_call | solution.py:259
  33.8 34.6 %forces.1 = (f32[6,64]{1,0:T(8,128)}, f32[6,64]{1,0:T(8,128)}, f32[6,64]{1,0:T(8,128)}) custom-call(f32[8192,128]{1,0:T(8,128)S(1)} %bitcast.4, f32[2,128,128]{2,1,0:T(8,128)S(1)} %get-tuple-element.8.req_ref, s32[64,128]{1,0:T(8,128)S(1)} %get-tuple-element.9.own_vec, f32[1024,128]{1,0:T(8,128)S(1)} %get-tuple-element.10.fetched, f32[6,64]{1,0:T(8,128)} %old_hbm.1), custom_call_target="tpu_custom_call" | custom-call | tf_op jit(solution)/shard_map/forces/pallas_call | solution.py:475
